TPU v7x, 32 devices: a whole 2x2x4 slice. The times are simulated.
32 devices in a mesh: seq: 8 (over z, x), head: 4 (over y, core).
Axes of the slice: x: 2, y: 2, z: 4, core: 2. Of those that a mesh axis runs over, the one named last changes fastest.
Arguments:
- tokens: bfloat16 [8192, 2048], P('seq', 'head'), may hold values from -6 to 6
- norm_gain: bfloat16 [2048], P('head'), may hold values from 0.5 to 1.5
- w_query: bfloat16 [2048, 2048], P(None, 'head'), may hold values from -0.125 to 0.125
- w_key: bfloat16 [2048, 2048], P(None, 'head'), may hold values from -0.125 to 0.125
- w_value: bfloat16 [2048, 3456], P(None, 'head'), may hold values from -0.125 to 0.125
- w_gate: bfloat16 [2048, 3456], P(None, 'head'), may hold values from -0.125 to 0.125
- group_gain: bfloat16 [3456], P('head'), may hold values from 0.5 to 1.5
- w_output: bfloat16 [3456, 2048], P('head'), may hold values from -0.109375 to 0.109375
- mlp_gain: bfloat16 [2048], P('head'), may hold values from 0.5 to 1.5
- w_first: bfloat16 [2048, 3456], P(None, 'head'), may hold values from -0.125 to 0.125
- w_second: bfloat16 [2048, 3456], P(None, 'head'), may hold values from -0.125 to 0.125
- w_third: bfloat16 [3456, 2048], P('head'), may hold values from -0.109375 to 0.109375
- cotangent: bfloat16 [8192, 2048], P('seq', 'head'), may hold values from -6 to 6
Outputs:
- output: bfloat16 [8192, 2048], P('seq', 'head')
- grad_tokens: bfloat16 [8192, 2048], P('seq', 'head')
- grad_norm_gain: float32 [2048], P('head')
- grad_query: float32 [2048, 2048], P(None, 'head')
- grad_key: float32 [2048, 2048], P(None, 'head')
- grad_value: float32 [2048, 3456], P(None, 'head')
- grad_gate: float32 [2048, 3456], P(None, 'head')
- grad_group_gain: float32 [3456], P('head')
- grad_output: float32 [3456, 2048], P('head')
- grad_mlp_gain: float32 [2048], P('head')
- grad_first: float32 [2048, 3456], P(None, 'head')
- grad_second: float32 [2048, 3456], P(None, 'head')
- grad_third: float32 [3456, 2048], P('head')
All inputs are finite; a program needn't handle non-finite values.
Results may differ from a plain program's by a relative error of at most 0.023.
Values may be sent and summed in bfloat16 or wider, within the bound.
A program may use at most 320 MiB of HBM per device.

v0:
```python
import math

import jax
import jax.numpy as jnp
from jax import lax
from jax.sharding import PartitionSpec as P

DK = 256
DV = 432
BLK = 512


highest_precision = lax.Precision.HIGHEST


def prefix(value, axis, join, neutral):
    count, mine = (lax.axis_size(axis), lax.axis_index(axis))
    pieces = jax.tree.map(lambda part: lax.all_gather(part, axis), value)
    total = jax.tree.map(
        lambda part, zero: jnp.full_like(part, 0) + jnp.asarray(zero, part.dtype), value, neutral
    )

    def prefix_lap(position, total):
        longer = join(total, jax.tree.map(lambda part: part[position], pieces))
        return jax.tree.map(lambda new, old: jnp.where(position < mine, new, old), longer, total)

    return lax.fori_loop(0, count - 1, prefix_lap, total)


def carried_in(shard, axis, combine, identity):
    peers, position = (lax.axis_size(axis), lax.axis_index(axis))
    everything = jax.tree.map(
        lambda part, kind: lax.all_gather(part.astype(kind), axis),
        shard,
        (jnp.bfloat16, jnp.bfloat16),
    )
    start = jax.tree.map(
        lambda part, zero: jnp.broadcast_to(jnp.asarray(zero, part.dtype), part.shape),
        shard,
        identity,
    )

    def carried_lap(k, before):
        at = peers - 1 - k
        reached = at > position
        new = combine(
            before, jax.tree.map(lambda part, own: part[at].astype(own.dtype), everything, shard)
        )
        return jax.tree.map(lambda a, b: jnp.where(reached, a, b), new, before)

    return lax.fori_loop(0, peers, carried_lap, start)


def contract(left_side, right_side, left_dim, right_dim):
    return lax.dot_general(
        left_side,
        right_side,
        (((left_dim,), (right_dim,)), ((), ())),
        preferred_element_type=jnp.float32,
    )


def row_stats(values, epsilon):
    centred = values - jnp.mean(values, axis=-1, keepdims=True)
    inverse = lax.rsqrt(jnp.mean(centred * centred, axis=-1, keepdims=True) + epsilon)
    return (centred * inverse, inverse)


def norm_back(grad_norm, normal_rows, inverse):
    return inverse * (
        grad_norm
        - jnp.mean(grad_norm, axis=-1, keepdims=True)
        - normal_rows * jnp.mean(grad_norm * normal_rows, axis=-1, keepdims=True)
    )


def rotate(values, cosine, sine_part):
    half_size = values.shape[-1] // 2
    first_half = values[..., :half_size]
    second_half = values[..., half_size:]
    return jnp.concatenate(
        [
            first_half * cosine - second_half * sine_part,
            second_half * cosine + first_half * sine_part,
        ],
        axis=-1,
    )


def gelu_parts(values):
    cumulative = 0.5 * (1.0 + jax.scipy.special.erf(values / math.sqrt(2.0)))
    density = jnp.exp(-0.5 * values * values) / math.sqrt(2.0 * math.pi)
    return (values * cumulative, cumulative + values * density)


def chain_combine(earlier, later):
    return (earlier[0] * later[0], later[0][:, None, None] * earlier[1] + later[1])


def decay_tables(log_decay):
    offsets = jnp.arange(BLK, dtype=jnp.float32)
    lagged = offsets[:, None] - offsets[None, :]
    causal = lagged >= 0
    decay_mask = jnp.where(
        causal[None], jnp.exp(jnp.where(causal, lagged, 0.0)[None] * log_decay[:, None, None]), 0.0
    )
    into_block = jnp.exp((offsets[:, None] + 1.0) * log_decay[None, :])
    output_block_rows = jnp.exp((BLK - 1.0 - offsets)[:, None] * log_decay[None, :])
    across = jnp.exp(BLK * log_decay)
    return (decay_mask, into_block, output_block_rows, across)


def split_blocks(values):
    return values.reshape(values.shape[0] // BLK, BLK, values.shape[1], values.shape[2])


def local_forward(queries, key_rows, value_rows, tables):
    decay_mask, into_block, output_block_rows, across = tables

    def one_block(state, pieces):
        query_block_rows, key_block_rows, value_block_rows = pieces
        attention_scores = jnp.einsum(
            "pvy,ovy->vpo", query_block_rows, key_block_rows, preferred_element_type=jnp.float32
        )
        weights = (attention_scores * decay_mask).astype(jnp.bfloat16)
        inner_part = jnp.einsum(
            "hnm,mhe->nhe", weights, value_block_rows, preferred_element_type=jnp.float32
        )
        carried = jnp.einsum(
            "nhd,hde->nhe",
            query_block_rows.astype(jnp.float32) * into_block[:, :, None],
            state,
            precision=highest_precision,
        )
        state_update = jnp.einsum(
            "zrb,zrg->rbg",
            key_block_rows.astype(jnp.float32) * output_block_rows[:, :, None],
            value_block_rows.astype(jnp.float32),
            precision=highest_precision,
        )
        return (across[:, None, None] * state + state_update, (inner_part + carried, state))

    initial_state = jnp.zeros(
        (queries.shape[1], queries.shape[2], value_rows.shape[2]), jnp.float32
    )
    final_state, (outputs, states) = lax.scan(
        one_block,
        initial_state,
        (split_blocks(queries), split_blocks(key_rows), split_blocks(value_rows)),
    )
    return (outputs.reshape(value_rows.shape), final_state, states)


def local_backward(queries, key_rows, value_rows, grad_out, states, grad_final, tables):
    decay_mask, into_block, output_block_rows, across = tables

    def one_block(carried_state_gradient, pieces):
        query_block_rows, key_block_rows, value_block_rows, g_block, state = pieces
        attention_scores = jnp.einsum(
            "pvy,ovy->vpo", query_block_rows, key_block_rows, preferred_element_type=jnp.float32
        )
        weights = (attention_scores * decay_mask).astype(jnp.bfloat16)
        grad_weights = jnp.einsum(
            "nhe,mhe->hnm", g_block, value_block_rows, preferred_element_type=jnp.float32
        )
        scores_gradient = (grad_weights * decay_mask).astype(jnp.bfloat16)
        g_wide = g_block.astype(jnp.float32)
        q_scaled = query_block_rows.astype(jnp.float32) * into_block[:, :, None]
        key_scaled_rows = key_block_rows.astype(jnp.float32) * output_block_rows[:, :, None]
        grad_query = (
            jnp.einsum(
                "car,rce->ace", scores_gradient, key_block_rows, preferred_element_type=jnp.float32
            )
            + jnp.einsum("nhe,hde->nhd", g_wide, state, precision=highest_precision)
            * into_block[:, :, None]
        )
        grad_key = (
            jnp.einsum(
                "pcg,cpe->gpe",
                scores_gradient,
                query_block_rows,
                preferred_element_type=jnp.float32,
            )
            + jnp.einsum(
                "zrl,rbl->zrb",
                value_block_rows.astype(jnp.float32),
                carried_state_gradient,
                precision=highest_precision,
            )
            * output_block_rows[:, :, None]
        )
        grad_value = jnp.einsum(
            "hnm,nhe->mhe", weights, g_block, preferred_element_type=jnp.float32
        ) + jnp.einsum(
            "afj,fjr->afr", key_scaled_rows, carried_state_gradient, precision=highest_precision
        )
        new_carry = across[:, None, None] * carried_state_gradient + jnp.einsum(
            "nhd,nhe->hde", q_scaled, g_wide, precision=highest_precision
        )
        return (new_carry, (grad_query, grad_key, grad_value))

    pieces = (
        split_blocks(queries),
        split_blocks(key_rows),
        split_blocks(value_rows),
        split_blocks(grad_out),
        states,
    )
    _, (grad_query, grad_key, grad_value) = lax.scan(one_block, grad_final, pieces, reverse=True)
    return (
        grad_query.reshape(queries.shape),
        grad_key.reshape(key_rows.shape),
        grad_value.reshape(value_rows.shape),
    )


def per_device(
    tokens,
    norm_gain,
    w_query,
    w_key,
    w_value,
    w_gate,
    group_gain,
    w_output,
    mlp_gain,
    w_first,
    w_second,
    w_third,
    cotangent,
):
    tok_rows = tokens.shape[0]
    col_count = tokens.shape[1]
    heads_here = w_query.shape[1] // DK
    value_cols = w_value.shape[1]
    head_rank = lax.axis_index("head")
    seq_rank = lax.axis_index("seq")
    feature_total = col_count * lax.axis_size("head")
    all_tokens, full_gain = (
        lax.all_gather(tokens, "head", axis=1, tiled=True),
        lax.all_gather(norm_gain, "head", axis=0, tiled=True),
    )
    normal_in, inverse_in = row_stats(all_tokens.astype(jnp.float32), 1e-05)
    normed = (normal_in * full_gain.astype(jnp.float32)).astype(jnp.bfloat16)
    query_raw = jnp.dot(normed, w_query, preferred_element_type=jnp.float32).reshape(
        tok_rows, heads_here, DK
    )
    key_raw = jnp.dot(normed, w_key, preferred_element_type=jnp.float32).reshape(
        tok_rows, heads_here, DK
    )
    value_rows = (
        jnp.dot(normed, w_value, preferred_element_type=jnp.float32)
        .astype(jnp.bfloat16)
        .reshape(tok_rows, heads_here, DV)
    )
    gate_raw = jnp.dot(normed, w_gate, preferred_element_type=jnp.float32)
    positions = (seq_rank * tok_rows + jnp.arange(tok_rows)).astype(jnp.float32)
    frequency = 10000.0 ** (-jnp.arange(DK // 2, dtype=jnp.float32) / (DK // 2 - 1))
    angles = positions[:, None] * frequency[None, :]
    cosine = jnp.cos(angles)[:, None, :]
    sine_part = jnp.sin(angles)[:, None, :]
    queries = rotate(query_raw, cosine, sine_part).astype(jnp.bfloat16)
    key_rows = (rotate(key_raw, cosine, sine_part) / math.sqrt(DK)).astype(jnp.bfloat16)
    head_ids = (head_rank * heads_here + jnp.arange(heads_here)).astype(jnp.float32)
    log_decay = jnp.log(1.0 - jnp.exp2(-5.0 - head_ids))
    tables = decay_tables(log_decay)
    into_device = jnp.exp(
        (jnp.arange(tok_rows, dtype=jnp.float32) + 1.0)[:, None] * log_decay[None, :]
    )
    factor = jnp.exp(tok_rows * log_decay)
    queries_scaled = queries.astype(jnp.float32) * into_device[:, :, None]
    local_out, local_end, local_states = local_forward(queries, key_rows, value_rows, tables)
    identity = (jnp.ones_like(factor), jnp.zeros_like(local_end))
    _, incoming = prefix((factor, local_end), "seq", chain_combine, identity)
    retained = local_out + jnp.einsum(
        "nhd,hde->nhe", queries_scaled, incoming, precision=highest_precision
    )
    normal_ret, inverse_ret = row_stats(retained, 0.5)
    gain_grid = group_gain.astype(jnp.float32).reshape(heads_here, DV)
    grouped = (normal_ret * gain_grid).reshape(tok_rows, value_cols)
    gate_sig = jax.nn.sigmoid(gate_raw)
    gate_act = gate_raw * gate_sig
    mixed_out = (gate_act * grouped).astype(jnp.bfloat16)
    branch_terms = jnp.dot(mixed_out, w_output, preferred_element_type=jnp.float32)
    branch_part = lax.psum_scatter(
        branch_terms.astype(jnp.bfloat16), "head", scatter_dimension=1, tiled=True
    ).astype(jnp.float32)
    residual = tokens.astype(jnp.float32) + branch_part
    all_resid, full_mlp_gain = (
        lax.all_gather(residual, "head", axis=1, tiled=True),
        lax.all_gather(mlp_gain.astype(jnp.float32), "head", axis=0, tiled=True),
    )
    normal_mid, inverse_mid = row_stats(all_resid, 1e-05)
    normed_two = (normal_mid * full_mlp_gain).astype(jnp.bfloat16)
    up_one = jnp.dot(normed_two, w_first, preferred_element_type=jnp.float32)
    up_two = jnp.dot(normed_two, w_second, preferred_element_type=jnp.float32)
    gelu_one, gelu_slope = gelu_parts(up_one)
    hidden = (gelu_one * up_two).astype(jnp.bfloat16)
    mlp_terms = jnp.dot(hidden, w_third, preferred_element_type=jnp.float32)
    mlp_part = lax.psum_scatter(
        mlp_terms.astype(jnp.bfloat16), "head", scatter_dimension=1, tiled=True
    ).astype(jnp.float32)
    output = (residual + mlp_part).astype(jnp.bfloat16)
    all_cot = lax.all_gather(cotangent, "head", axis=1, tiled=True)
    grad_third = contract(hidden, all_cot, 0, 0)
    grad_hidden = contract(all_cot, w_third, 1, 1)
    grad_up_one = (grad_hidden * up_two * gelu_slope).astype(jnp.bfloat16)
    grad_up_two = (grad_hidden * gelu_one).astype(jnp.bfloat16)
    grad_first = contract(normed_two, grad_up_one, 0, 0)
    grad_second = contract(normed_two, grad_up_two, 0, 0)
    norm_terms = contract(grad_up_one, w_first, 1, 1) + contract(grad_up_two, w_second, 1, 1)
    grad_normed_two = lax.psum(norm_terms.astype(jnp.bfloat16), "head").astype(jnp.float32)
    grad_gain_full = jnp.sum(grad_normed_two * normal_mid, axis=0)
    grad_mlp_gain = lax.dynamic_slice_in_dim(grad_gain_full, head_rank * col_count, col_count)
    grad_resid = all_cot.astype(jnp.float32) + norm_back(
        grad_normed_two * full_mlp_gain, normal_mid, inverse_mid
    )
    grad_branch = grad_resid.astype(jnp.bfloat16)
    own_resid_grad = lax.dynamic_slice_in_dim(grad_resid, head_rank * col_count, col_count, axis=1)
    grad_output = contract(mixed_out, grad_branch, 0, 0)
    grad_mixed = contract(grad_branch, w_output, 1, 1)
    grad_grouped = (grad_mixed * gate_act).reshape(tok_rows, heads_here, DV)
    grad_group_gain = jnp.sum(grad_grouped * normal_ret, axis=0).reshape(value_cols)
    grad_gate_rows = (grad_mixed * grouped * gate_sig * (1.0 + gate_raw * (1.0 - gate_sig))).astype(
        jnp.bfloat16
    )
    grad_retained = norm_back(grad_grouped * gain_grid, normal_ret, inverse_ret).astype(
        jnp.bfloat16
    )
    state_grad = jnp.einsum(
        "nhd,nhe->hde",
        queries_scaled,
        grad_retained.astype(jnp.float32),
        precision=highest_precision,
    )
    _, outgoing = carried_in((factor, state_grad), "seq", chain_combine, identity)
    block_count = tok_rows // BLK
    block_lift = jnp.exp(
        (jnp.arange(block_count, dtype=jnp.float32) * BLK)[:, None] * log_decay[None, :]
    )
    total_states = local_states + block_lift[:, :, None, None] * incoming[None]
    grad_query_rot, grad_key_rot, grad_value_rows = local_backward(
        queries, key_rows, value_rows, grad_retained, total_states, outgoing, tables
    )
    grad_query_raw = (
        rotate(grad_query_rot, cosine, -sine_part)
        .astype(jnp.bfloat16)
        .reshape(tok_rows, heads_here * DK)
    )
    grad_key_raw = (
        (rotate(grad_key_rot, cosine, -sine_part) / math.sqrt(DK))
        .astype(jnp.bfloat16)
        .reshape(tok_rows, heads_here * DK)
    )
    grad_value_low = grad_value_rows.astype(jnp.bfloat16).reshape(tok_rows, value_cols)
    grad_query = contract(normed, grad_query_raw, 0, 0)
    grad_key = contract(normed, grad_key_raw, 0, 0)
    grad_value = contract(normed, grad_value_low, 0, 0)
    grad_gate = contract(normed, grad_gate_rows, 0, 0)
    input_terms = contract(grad_query_raw, w_query, 1, 1) + contract(grad_key_raw, w_key, 1, 1)
    input_terms = (
        input_terms
        + contract(grad_value_low, w_value, 1, 1)
        + contract(grad_gate_rows, w_gate, 1, 1)
    )
    grad_normed = lax.psum_scatter(
        input_terms.astype(jnp.bfloat16), "head", scatter_dimension=1, tiled=True
    ).astype(jnp.float32)
    own_normal = lax.dynamic_slice_in_dim(normal_in, head_rank * col_count, col_count, axis=1)
    scaled_grad = grad_normed * norm_gain.astype(jnp.float32)
    sum_plain, sum_cross = lax.psum(
        (jnp.sum(scaled_grad, axis=1), jnp.sum(scaled_grad * own_normal, axis=1)), "head"
    )
    grad_tokens = (
        own_resid_grad
        + inverse_in
        * (scaled_grad - (sum_plain[:, None] + own_normal * sum_cross[:, None]) / feature_total)
    ).astype(jnp.bfloat16)
    grad_norm_gain = jnp.sum(grad_normed * own_normal, axis=0)
    (
        grad_norm_gain,
        grad_query,
        grad_key,
        grad_value,
        grad_gate,
        grad_group_gain,
        grad_output,
        grad_mlp_gain,
        grad_first,
        grad_second,
        grad_third,
    ) = (
        lax.psum(grad_norm_gain.astype(jnp.bfloat16), "seq").astype(jnp.float32),
        lax.psum(grad_query.astype(jnp.bfloat16), "seq").astype(jnp.float32),
        lax.psum(grad_key.astype(jnp.bfloat16), "seq").astype(jnp.float32),
        lax.psum(grad_value.astype(jnp.bfloat16), "seq").astype(jnp.float32),
        lax.psum(grad_gate.astype(jnp.bfloat16), "seq").astype(jnp.float32),
        lax.psum(grad_group_gain.astype(jnp.bfloat16), "seq").astype(jnp.float32),
        lax.psum(grad_output.astype(jnp.bfloat16), "seq").astype(jnp.float32),
        lax.psum(grad_mlp_gain.astype(jnp.bfloat16), "seq").astype(jnp.float32),
        lax.psum(grad_first.astype(jnp.bfloat16), "seq").astype(jnp.float32),
        lax.psum(grad_second.astype(jnp.bfloat16), "seq").astype(jnp.float32),
        lax.psum(grad_third.astype(jnp.bfloat16), "seq").astype(jnp.float32),
    )
    return (
        output,
        grad_tokens,
        grad_norm_gain,
        grad_query,
        grad_key,
        grad_value,
        grad_gate,
        grad_group_gain,
        grad_output,
        grad_mlp_gain,
        grad_first,
        grad_second,
        grad_third,
    )


def solution(mesh):
    placed = (
        P("seq", "head"),
        P("head"),
        P(None, "head"),
        P(None, "head"),
        P(None, "head"),
        P(None, "head"),
        P("head"),
        P("head", None),
        P("head"),
        P(None, "head"),
        P(None, "head"),
        P("head", None),
        P("seq", "head"),
    )
    return jax.shard_map(
        per_device,
        mesh=mesh,
        in_specs=placed,
        out_specs=(
            P("seq", "head"),
            P("seq", "head"),
            P("head"),
            P(None, "head"),
            P(None, "head"),
            P(None, "head"),
            P(None, "head"),
            P("head"),
            P("head", None),
            P("head"),
            P(None, "head"),
            P(None, "head"),
            P("head", None),
        ),
        check_vma=False,
    )
```

profile of v0, /device:TPU:0, one launch (start us, length us, event | category | flops | bytes accessed | tf_op | source)
XLA Modules:
  0.0 1705.2 jit_solution(7079181494513999399)
XLA Ops:
  8.9 6.1 all-gather.2
  21.0 25.8 %all-gather.12.cloned.1.call-done = bf16[1024,2048]{1,0:T(8,128)(2,1)} async-done(((bf16[1024,512]{1,0:T(8,128)(2,1)}), bf16[1024,2048]{1,0:T(8,128)(2,1)}) %all-gather.12.cloned.1.call-update) | async-done | bytes 4194320 | tf_op jit(solution)/shard_map/all_gather | solution.py:240
  64.7 5.2 fusion.156
  76.6 8.3 convolution_convert_fusion.10
  84.9 5.5 reshape_reshape.4
  98.1 96.4 %while.72 = (s32[]{:T(128)}, f32[2,256,432]{1,2,0:T(8,128)}, f32[2,512,2,432]{1,0,3,2:T(2,128)}, f32[2,2,256,432]{2,3,1,0:T(8,128)}, bf16[2,512,2,256]{3,1,0,2:T...) while((s32[]{:T(128)}, f32[2,256,432]{1,2,0:T(8,128)}, ...), condition=%wide.region_3.4_spmd.clone.clone.clone, body=%wide.region_2.3_spmd.clone.clone.clone.sunk | while | flops 3444025344 | bytes 29089508 | solution.py:146
  113.1 32.4 %dynamic_update_slice.59 = f32[2,512,2,432]{1,0,3,2:T(2,128)} dynamic-update-slice(f32[2,512,2,432]{1,0,3,2:T(2,128)} %get-tuple-element.1355, f32[1,512,2,432]{1,0,3,2:T(1,128)} %copy.166, s32[]{:T(128)S(6)} %copy.176, s32[]{:T(128)} %constant.178.clone.1..sunk.2, s32[]{:T(128)} %constant.178.clone.1..sunk.2, s32[]{:T(128)} %constant.178.clone.1..sunk.2) | dynamic-update-slice | bytes 3538948 | tf_op jit(solution)/shard_map/while/body/jit(dynamic_update_index_in_dim)/dynamic_update_slice | solution.py:146
  162.1 32.4 %dynamic_update_slice.59 = f32[2,512,2,432]{1,0,3,2:T(2,128)} dynamic-update-slice(f32[2,512,2,432]{1,0,3,2:T(2,128)} %get-tuple-element.1355, f32[1,512,2,432]{1,0,3,2:T(1,128)} %copy.166, s32[]{:T(128)S(6)} %copy.176, s32[]{:T(128)} %constant.178.clone.1..sunk.2, s32[]{:T(128)} %constant.178.clone.1..sunk.2, s32[]{:T(128)} %constant.178.clone.1..sunk.2) | dynamic-update-slice | bytes 3538948 | tf_op jit(solution)/shard_map/while/body/jit(dynamic_update_index_in_dim)/dynamic_update_slice | solution.py:146
  194.6 20.8 %all-gather.3 = f32[8,1,2]{2,1,0:T(1,128)} all-gather(f32[1,1,2]{2,1,0:T(1,128)S(1)} %fusion.150), channel_id=1, replica_groups=mesh['seq'=8,'head'=4] {'seq'}, dimensions={0}, use_global_device_ids=true | all-gather | bytes 72 | tf_op jit(solution)/shard_map/all_gather | solution.py:18
  216.8 5.8 reshape.381
  222.6 80.9 %all-gather.18.cloned.1.call-done = f32[16,256,432]{1,2,0:T(8,128)} async-done(((f32[2,256,432]{1,2,0:T(8,128)}), f32[16,256,432]{1,2,0:T(8,128)}) %all-gather.18.cloned.1.call-update) | async-done | bytes 7077904 | tf_op jit(solution)/shard_map/all_gather | solution.py:18
  303.5 60.4 %while.69 = (s32[]{:T(128)}, f32[2,256,432]{2,1,0:T(8,128)}, s32[]{:T(128)}, f32[8,2]{1,0:T(8,128)}, f32[8,2,256,432]{2,3,1,0:T(8,128)}, /*index=5*/s32[]{:T(128)}, s32[]{:T(128)}) while((s32[]{:T(128)}, f32[2,256,432]{2,1,0:T(8,128)}, s32[]{:T(128)}, f32[8,2]{1,0:T(8,128)}, f32[8,2,256,432]{2,3,1,0:T(8,128)}, ...), condition=%wide.region_5.6_spmd.clone, body=%wide.region_4.5_spmd.clone.sunk | while | flops 884740 | bytes 6193289 | solution.py:27
  364.0 10.0 fusion.155
  378.7 6.0 fusion.122
  386.0 6.3 convolution_convert_fusion.1
  392.4 42.8 %reduce-scatter.4.cloned.1.call-done = bf16[1024,512]{1,0:T(8,128)(2,1)} async-done(((bf16[1024,2048]{1,0:T(8,128)(2,1)}), bf16[1024,512]{1,0:T(8,128)(2,1)}) %reduce-scatter.4.cloned.1.call-update) | async-done | bytes 1048592 | tf_op jit(solution)/shard_map/reduce_scatter | solution.py:285
  439.7 5.5 all-gather.4
  445.2 51.6 %all-gather.14.cloned.1.call-done = f32[1024,2048]{1,0:T(8,128)} async-done(((f32[1024,512]{1,0:T(8,128)}), f32[1024,2048]{1,0:T(8,128)}) %all-gather.14.cloned.1.call-update) | async-done | bytes 8388624 | tf_op jit(solution)/shard_map/all_gather | solution.py:290
  496.8 4.4 reduce_sum.139
  502.0 4.9 multiply_reduce_fusion
  511.1 5.7 fusion.158
  516.9 5.7 fusion.159
  522.6 10.2 all-gather.16.cloned.1.call-done
  532.9 9.8 multiply_convert_fusion.3
  542.8 4.6 fusion.160
  547.4 6.4 add_convert_fusion.1
  553.9 85.6 %all-reduce.6.cloned.1.call-done = bf16[1024,2048]{1,0:T(8,128)(2,1)} async-done(((bf16[1024,2048]{1,0:T(8,128)(2,1)}), bf16[1024,2048]{1,0:T(8,128)(2,1)}) %all-reduce.6.cloned.1.call-update) | async-done | bytes 4194320 | tf_op jit(solution)/shard_map/psum | solution.py:312
  639.5 7.6 fusion.115
  647.1 5.8 fusion.113
  652.9 11.6 fusion.148
  671.4 20.5 %all-gather.5 = bf16[8,1,2]{2,1,0:T(2,128)(2,1)S(1)} all-gather(bf16[1,1,2]{2,1,0:T(2,128)(2,1)S(1)} %convert_bitcast_fusion), channel_id=1, replica_groups=mesh['seq'=8,'head'=4] {'seq'}, dimensions={0}, use_global_device_ids=true | all-gather | bytes 36 | tf_op jit(solution)/shard_map/all_gather | solution.py:33
  698.3 6.3 convolution_convert_fusion
  706.6 8.5 fusion.163
  716.5 20.3 %all-gather.20.cloned.1.call-done = bf16[16,256,432]{1,2,0:T(8,128)(2,1)} async-done(((bf16[2,256,432]{1,2,0:T(8,128)(2,1)}), bf16[16,256,432]{1,2,0:T(8,128)(2,1)}) %all-gather.20.cloned.1.call-update) | async-done | bytes 3538960 | tf_op jit(solution)/shard_map/all_gather | solution.py:33
  736.8 15.3 while.70
  756.8 56.6 %while.71 = (s32[]{:T(128)}, f32[2,256,432]{1,2,0:T(8,128)S(1)}, f32[2,512,2,256]{3,1,0,2:T(8,128)}, f32[2,512,2,256]{3,1,0,2:T(8,128)}, bf16[2,512,2,432]{1,3,2...) while((s32[]{:T(128)}, f32[2,256,432]{1,2,0:T(8,128)S(1)}, ...), condition=%wide.region_20.21_spmd.clone.clone, body=%wide.region_19.20_spmd.clone.clone.sunk | while | flops 7154272256 | bytes 57015080 | solution.py:209
  823.9 7.7 fusion.161
  831.7 6.9 fusion.162
  838.6 12.7 add_convert_fusion
  852.7 8.0 convolution_convert_fusion.3
  860.7 5.2 convolution_convert_fusion.2
  866.0 5.3 convolution_convert_fusion.6
  871.3 5.3 convolution_convert_fusion.4
  876.6 5.4 convolution_convert_fusion.7
  889.6 5.3 convolution_convert_fusion.5
  901.9 20.0 %all-reduce.1 = (bf16[512]{0:T(512)(128)(2,1)S(1)}, bf16[864]{0:T(1024)(128)(2,1)S(1)}, bf16[512]{0:T(512)(128)(2,1)S(1)}) all-reduce(bf16[512]{0:T(512)(128)(2,1)S(1)} %get-tuple-element.952, bf16[864]{0:T(1024)(128)(2,1)S(1)} %convert_element_type.347, bf16[512]{0:T(512)(128)(2,1)S(1)} %dynamic_slice.191), channel_id=1, replica_groups=mesh['seq'=8,'head'=4] {'seq'}, use_global_device_ids=true, to_apply=%region_27.28 | all-reduce | flops 1888 | bytes 7552 | tf_op jit(solution)/shard_map/psum | solution.py:393
  923.6 6.1 all-reduce
  933.5 733.9 %all-reduce.8.cloned.1.call-done = (bf16[2048,512]{1,0:T(8,128)(2,1)}, bf16[2048,512]{1,0:T(8,128)(2,1)}, bf16[2048,864]{0,1:T(8,128)(2,1)}, bf16[2048,864]{0,1:...) async-done(((bf16[2048,512]{1,0:T(8,128)(2,1)}, bf16[2048,512]{1,0:T(8,128)(2,1)}, ...) | async-done | bytes 25427984 | tf_op jit(solution)/shard_map/psum | solution.py:394
  (418 shorter events, 303.5 us)
Async XLA Ops:
  7.2 525.7 %copy-start = (bf16[864,2048]{1,0:T(8,128)(2,1)S(1)}, bf16[864,2048]{1,0:T(8,128)(2,1)}, u32[]{:S(2)}) copy-start(bf16[864,2048]{1,0:T(8,128)(2,1)} %param.32) | copy-start | bytes 10616836
  7.2 39.6 %all-gather.12.cloned.1.call-start = ((), (), s32[]{:S(2)}) async-start(), calls=%async_computation.3 | async-start | bytes 5242880 | tf_op jit(solution)/shard_map/all_gather | solution.py:240
  7.9 295.6 %all-gather.18.cloned.1.call-start = ((), (), s32[]{:S(2)}) async-start(), calls=%async_computation.10 | async-start | bytes 7962624 | tf_op jit(solution)/shard_map/all_gather | solution.py:18
  98.1 117.4 %copy-start.67 = (bf16[864]{0:T(1024)(128)(2,1)S(1)}, bf16[864]{0:T(1024)(128)(2,1)}, u32[]{:S(2)}) copy-start(bf16[864]{0:T(1024)(128)(2,1)} %param.27) | copy-start | bytes 5188
  194.5 28.1 %copy-start.55 = (f32[2]{0:T(128)}, f32[2]{0:T(128)S(1)}, u32[]{:S(2)}) copy-start(f32[2]{0:T(128)S(1)} %get-tuple-element.1553) | copy-start | bytes 28
  194.5 240.7 %reduce-scatter.4.cloned.1.call-start = ((), (), s32[]{:S(2)}) async-start(), calls=%async_computation.4 | async-start | bytes 5242880 | tf_op jit(solution)/shard_map/reduce_scatter | solution.py:285
  303.5 60.4 %copy-start.63 = (f32[1024,2]{0,1:T(2,128)S(1)}, f32[1024,2]{0,1:T(2,128)}, u32[]{:S(2)}) copy-start(f32[1024,2]{0,1:T(2,128)} %multiply_exponential_fusion.6) | copy-start | bytes 24580
  378.7 6.0 copy-start.35
  378.7 7.2 copy-start.73
  392.3 104.5 %all-gather.14.cloned.1.call-start = ((), (), s32[]{:S(2)}) async-start(), calls=%async_computation.5 | async-start | bytes 10485760 | tf_op jit(solution)/shard_map/all_gather | solution.py:290
  438.4 94.4 %all-gather.16.cloned.1.call-start = ((), (), s32[]{:S(2)}) async-start(), calls=%async_computation.7 | async-start | bytes 5242880 | tf_op jit(solution)/shard_map/all_gather | solution.py:304
  439.0 200.5 %all-reduce.6.cloned.1.call-start = ((), (), s32[]{:S(2)}) async-start(), calls=%async_computation.8 | async-start | bytes 8388608 | tf_op jit(solution)/shard_map/psum | solution.py:312
  502.0 7.2 copy-start.2
  502.0 7.2 copy-start.50
  511.1 5.8 copy-start.28
  511.1 5.8 copy-start.71
  532.9 9.9 copy-start.70
  553.9 183.0 %all-gather.20.cloned.1.call-start = ((), (), s32[]{:S(2)}) async-start(), calls=%async_computation.11 | async-start | bytes 3981312 | tf_op jit(solution)/shard_map/all_gather | solution.py:33
  639.5 7.6 copy-start.10
  639.5 7.6 copy-start.26
  639.5 7.6 copy-start.51
  647.1 5.8 copy-start.36
  652.9 11.7 copy-start.11
  652.9 11.6 copy-start.4
  652.9 11.6 copy-start.53
  652.9 11.6 copy-start.58
  668.6 23.9 %copy-start.56 = (f32[2]{0:T(128)S(1)}, f32[2]{0:T(128)}, u32[]{:S(2)}) copy-start(f32[2]{0:T(128)} %copy-done.55) | copy-start | bytes 28
  671.3 225.1 %reduce-scatter.6.cloned.1.call-start = ((), (), s32[]{:S(2)}) async-start(), calls=%async_computation.6 | async-start | bytes 5242880 | tf_op jit(solution)/shard_map/reduce_scatter | solution.py:300
  704.7 194.4 %reduce-scatter.8.cloned.1.call-start = ((), (), s32[]{:S(2)}) async-start(), calls=%async_computation.9 | async-start | bytes 5242880 | tf_op jit(solution)/shard_map/reduce_scatter | solution.py:366
  706.6 8.5 copy-start.16
  715.1 21.7 %copy-start.9 = (f32[2,256,432]{2,1,0:T(8,128)S(1)}, f32[2,256,432]{2,1,0:T(8,128)}, u32[]{:S(2)}) copy-start(f32[2,256,432]{2,1,0:T(8,128)} %custom-call.2) | copy-start | bytes 2654212
  715.1 21.7 %copy-start.68 = (bf16[8,1,2]{0,2,1:T(2,128)(2,1)S(1)}, bf16[8,1,2]{0,2,1:T(2,128)(2,1)}, u32[]{:S(2)}) copy-start(bf16[8,1,2]{0,2,1:T(2,128)(2,1)} %copy.94) | copy-start | bytes 100
  823.9 7.8 copy-start.47
  823.9 7.8 copy-start.76
  831.7 6.9 copy-start.43
  851.3 816.1 %all-reduce.8.cloned.1.call-start = ((), (), s32[]{:S(2)}) async-start(), calls=%async_computation.12 | async-start | bytes 50855936 | tf_op jit(solution)/shard_map/psum | solution.py:394
  852.7 8.0 copy-start.29
  852.7 8.0 copy-start.82
  860.7 5.3 copy-start.27
  860.7 5.2 copy-start.84
  866.0 5.3 copy-start.25
  866.0 5.3 copy-start.80
  866.0 10.6 slice-start
  871.3 5.3 slice-start.1
  871.3 5.3 copy-start.86
  876.6 5.4 copy-start.49
  896.5 33.3 %copy-start.61 = (f32[1024]{0:T(1024)S(1)}, f32[1024]{0:T(1024)}, u32[]{:S(2)}) copy-start(f32[1024]{0:T(1024)} %copy-done.60) | copy-start | bytes 12292
  899.1 30.7 %copy-start.30 = (bf16[1024,512]{1,0:T(8,128)(2,1)S(1)}, bf16[1024,512]{1,0:T(8,128)(2,1)}, u32[]{:S(2)}) copy-start(bf16[1024,512]{1,0:T(8,128)(2,1)} %reduce-scatter.8.cloned.1.call-done) | copy-start | bytes 3145732
  (54 other events, 172.5 us)
Sparse Core Ops, SparseCore 0:
  9.6 37.1 all-gather.11
  194.7 108.7 all-gather.17
  392.5 42.7 reduce-scatter.3
  438.5 58.2 all-gather.13
  498.3 34.4 all-gather.15
  554.0 85.4 all-reduce.5
  671.5 65.3 all-gather.19
  739.9 43.0 reduce-scatter.5
  851.4 43.4 reduce-scatter.7
  901.8 765.5 all-reduce.7
where the time goes:
time: 1720 us; the launch traced here: 1710 us
  waiting for transfers between devices  1050 us (61%)
  matrix products  235 us (14%)
  local copies, waits for them, and re-layouts  196 us (11%)
  other arithmetic  126 us (7%)
  blocking collectives  79.1 us (5%)
    psum x1, waiting for transfers between devices, per_device(): lax.psum(grad_query.astype(jnp.bfloat16), 'seq').astype(jnp.float32)  734 us
    dot_general x16, matrix products, contract(): lax.dot_general(left_side, right_side, (((left_dim,), (right_dim,)), ((),...  110 us
    psum x1, waiting for transfers between devices, per_device(): lax.psum(norm_terms.astype(jnp.bfloat16), 'head').astype(jnp.float32)  85.6 us
    all_gather x1, waiting for transfers between devices, prefix(): pieces = jax.tree.map(lambda part: lax.all_gather(part, axis), value)  80.9 us
    dynamic_update_slice x4, local copies, waits for them, and re-layouts, local_forward(): lax.scan(one_block, initial_state, (split_blocks(queries), split_blocks(k...  70.8 us
    all_gather x1, waiting for transfers between devices, per_device(): lax.all_gather(residual, 'head', axis=1, tiled=True)  51.6 us
    reduce_scatter x1, waiting for transfers between devices, per_device(): lax.psum_scatter(branch_terms.astype(jnp.bfloat16), 'head', scatter_dimen...  42.8 us
  transfers between devices with their start and end apart: 10, of which 8 were waited for; matrix products, arithmetic and copies ran while one was open for 13% of the time, Pallas kernels for 0%

commit v1 on v0

v1 whole, which is shorter than its diff:
```python
import functools
import math

import jax
import jax.numpy as jnp
from jax import lax
from jax.experimental import pallas as pl
from jax.experimental.pallas import tpu as pltpu
from jax.sharding import PartitionSpec as P

DK = 256
DV = 432
DVP = 512
BLK = 512
F32 = jnp.float32
BF16 = jnp.bfloat16


def contract(left_side, right_side, left_dim, right_dim):
    return lax.dot_general(
        left_side,
        right_side,
        (((left_dim,), (right_dim,)), ((), ())),
        preferred_element_type=F32,
    )


def row_stats(values, epsilon):
    centred = values - jnp.mean(values, axis=-1, keepdims=True)
    inverse = lax.rsqrt(jnp.mean(centred * centred, axis=-1, keepdims=True) + epsilon)
    return (centred * inverse, inverse)


def gelu_parts(values):
    cumulative = 0.5 * (1.0 + jax.scipy.special.erf(values / math.sqrt(2.0)))
    density = jnp.exp(-0.5 * values * values) / math.sqrt(2.0 * math.pi)
    return (values * cumulative, cumulative + values * density)


def head_reduce_scatter(terms):
    return lax.psum_scatter(terms.astype(BF16), "head", scatter_dimension=1, tiled=True).astype(F32)


def head_allreduce(terms):
    return lax.psum(terms.astype(BF16), "head").astype(F32)


def seq_carry(state, factor, reverse):
    n, me = lax.axis_size("seq"), lax.axis_index("seq")
    pieces = lax.all_gather(state.astype(BF16), "seq")
    total = jnp.zeros_like(state)
    for k in range(n):
        at = n - 1 - k if reverse else k
        longer = factor[:, None, None] * total + pieces[at].astype(F32)
        total = jnp.where((at > me) if reverse else (at < me), longer, total)
    return total


CHUNK = 16
PACE = 3
PIECE = 32
PIECES = -(-DV // PIECE)
LAG = 2
MESH = pl.DeviceIdType.MESH


def chain_kernel(
    n,
    small_h, hid_h, cot_h, mixed_h, branch_h, d1_h, d2_h, d1_far_h, d2_far_h, mid_h, mid_far_h, near_h, far_h,
    in_h, in_far_h,
    full_ref,
    g_ref, land_ref, cross_ref, wide_a, wide_b, slab_a, slab_b, give, take,
    load_sem, give_sem, take_sem, cross_sem, cross_sent, recv_sem, back_sem, send_sem, far_sem, side_sem, near_sem, own_sem,
):
    s = lax.axis_index("seq")
    z, x = s // 2, s % 2
    partner = s + 1 - 2 * x
    T, D = mid_h.shape

    def half(i):
        return pl.ds(pl.multiple_of(i * DVP, 128), DVP)

    def load(k, src, dst):
        return pltpu.make_async_copy(src, dst, load_sem.at[k])

    small = pl.ds(7 * DV + 2 * DK, 16)
    whole = 2 * DV // CHUNK
    loads_third = [
        load(0, hid_h, slab_a.at[0]), load(1, cot_h, wide_a.at[0]), load(14, small_h, g_ref.at[small]),
    ]
    loads_out = [load(2, mixed_h, slab_b.at[0, :, pl.ds(0, 2 * DVP)]), load(3, branch_h, wide_b)]
    loads_mid = [
        load(4, d1_h.at[:, half(x)], slab_a.at[0, :, pl.ds(0, DVP)]),
        load(5, d2_h.at[:, half(x)], slab_a.at[0, :, pl.ds(DVP, DVP)]),
        load(6, d1_far_h, slab_a.at[1, :, pl.ds(0, DVP)]),
        load(7, d2_far_h, slab_a.at[1, :, pl.ds(DVP, DVP)]),
        load(8, mid_h, wide_a.at[0]), load(9, mid_far_h, wide_a.at[1]),
    ]
    loads_in = [
        load(10, near_h, slab_b.at[0]), load(11, far_h, slab_b.at[1]), load(12, in_h, wide_a.at[0]),
        load(13, in_far_h, wide_a.at[1]),
    ]
    for copy in loads_third + loads_out:
        copy.start()
    spare = 2 * n * CHUNK - small.start - small.size
    if spare:
        g_ref[pl.ds(small.start + small.size, spare), :] = jnp.zeros((spare, D), BF16)

    greet((), partner)

    def chunk(j):
        return pl.ds(pl.multiple_of(j * CHUNK, 16), CHUNK)

    def remote(src, dst, send, recv, to):
        return pltpu.make_async_remote_copy(
            src_ref=src, dst_ref=dst, send_sem=send, recv_sem=recv,
            device_id={"seq": to}, device_id_type=MESH,
        )

    def pump(t):
        for flow in range(2):
            p = z if flow == 0 else 3 - z
            ahead = s + 2 if flow == 0 else s - 2
            behind = s - 2 if flow == 0 else s + 2
            i = t - LAG * p
            j = 2 * i + flow
            live = (i >= 0) & (i < n)

            @pl.when(live & (p == 0))
            def _():
                remote(g_ref.at[chunk(j)], land_ref.at[chunk(j)], send_sem.at[flow],
                       recv_sem.at[j], ahead).start()

            @pl.when(live & (p > 0))
            def _():
                pltpu.make_async_copy(land_ref.at[chunk(j)], land_ref.at[chunk(j)], recv_sem.at[j]).wait()
                land_ref[chunk(j), :] = (
                    land_ref[chunk(j), :].astype(F32) + g_ref[chunk(j), :].astype(F32)
                ).astype(BF16)

            @pl.when(live & (p > 0) & (p < 3))
            def _():
                remote(land_ref.at[chunk(j)], land_ref.at[chunk(j)], send_sem.at[flow],
                       recv_sem.at[j], ahead).start()

            @pl.when(live & (p == 3) & (j >= whole))
            def _():
                remote(land_ref.at[chunk(j)], full_ref.at[x, chunk(j)], far_sem.at[flow],
                       back_sem.at[j], behind).start()
                remote(land_ref.at[chunk(j)], full_ref.at[x, chunk(j)], side_sem.at[flow],
                       near_sem, partner).start()
                pltpu.make_async_copy(
                    land_ref.at[chunk(j)], full_ref.at[x, chunk(j)], own_sem
                ).start()

            @pl.when(live & (p == 3) & (j < whole))
            def _():
                remote(land_ref.at[chunk(j)], cross_ref.at[chunk(i)], cross_sent, cross_sem.at[i], partner).start()

            i1 = i - 1
            j1 = 2 * i1 + flow

            @pl.when((i1 >= 0) & (p == 3) & (j1 < whole))
            def _():
                here = cross_ref.at[chunk(i1)]
                pltpu.make_async_copy(here, here, cross_sem.at[i1]).wait()
                cross_ref[chunk(i1), :] = (
                    cross_ref[chunk(i1), :].astype(F32) + land_ref[chunk(j1), :].astype(F32)
                ).astype(BF16)
                remote(here, full_ref.at[x, chunk(j1)], far_sem.at[flow], back_sem.at[j1], behind).start()
                pltpu.make_async_copy(here, full_ref.at[x, chunk(j1)], own_sem).start()

            i2 = t - 6 * LAG - 1 + LAG * p
            j2 = 2 * i2 + flow
            live2 = (i2 >= 0) & (i2 < n) & (p < 3)

            @pl.when(live2)
            def _():
                pltpu.make_async_copy(
                    land_ref.at[chunk(j2)], full_ref.at[x, chunk(j2)], back_sem.at[j2]
                ).wait()

            @pl.when(live2 & (j2 >= whole))
            def _():
                remote(full_ref.at[x, chunk(j2)], full_ref.at[x, chunk(j2)], side_sem.at[flow],
                       near_sem, partner).start()

            @pl.when(live2 & (p > 0))
            def _():
                remote(full_ref.at[x, chunk(j2)], full_ref.at[x, chunk(j2)], far_sem.at[flow],
                       back_sem.at[j2], behind).start()

    def unit(u):
        return pl.ds(pl.multiple_of(DV * (u // 4) + 128 * (u % 4), 16), 128)

    def columns(k):
        return pl.ds(pl.multiple_of(k * 128, 128), 128)

    def block(u):
        return pl.ds(pl.multiple_of(u * 128, 128), 128)

    def piece(k):
        return pl.ds(pl.multiple_of(k * PIECE, 32), PIECE)

    def trade(k):
        return remote(give.at[piece(k)], take.at[piece(k)], give_sem.at[k], take_sem.at[k], partner)

    def taken(u, size):
        for k in range(size // PIECE if size == 128 else 2):
            here = take.at[piece(4 * u + k)]
            pltpu.make_async_copy(here, here, take_sem.at[4 * u + k]).wait()
        mine = pl.ds(pl.multiple_of(4 * DV + 128 * u, 16), size)
        theirs = pl.ds(pl.multiple_of(u * 128, 128), size)
        g_ref[mine, :] = (g_ref[mine, :].astype(F32) + take[theirs, :].astype(F32)).astype(BF16)

    def both(slab, wide, k):
        near = contract(slab[0, :, columns(k)], wide[0], 0, 0)
        return (near + contract(slab[1, :, columns(k)], wide[1], 0, 0)).astype(BF16)

    def alone(k, wide):
        return contract(k, wide, 0, 0).astype(BF16)

    for copy in loads_third:
        copy.wait()
    g_ref[unit(0), :] = alone(slab_a[0, :, columns(0)], wide_a[0])

    def step(t, carry):
        tick = t // PACE
        beat = t % PACE == 0
        u = tick - 14

        @pl.when(beat & (u >= 0) & (u < 3))
        def _():
            taken(u, 128)

        @pl.when(beat & (u == 3))
        def _():
            taken(3, DV - 384)

        pump(t)

        @pl.when(beat & (tick == 0))
        def _():
            for copy in loads_out:
                copy.wait()

        @pl.when(beat & (tick < 6))
        def _():
            g_ref[unit(1 + tick), :] = alone(slab_a[0, :, columns(1 + tick)], wide_a[0])

        @pl.when(beat & (tick == 6))
        def _():
            last = alone(slab_a[0, :, columns(7)], wide_a[0])
            g_ref[pl.ds(DV + 384, DV - 384), :] = last[: DV - 384]

        @pl.when(beat & (tick < 4))
        def _():
            give[block(tick), :] = alone(slab_b[0, :, columns((1 - x) * 4 + tick)], wide_b[...])
            g_ref[unit(16 + tick), :] = alone(slab_b[0, :, columns(x * 4 + tick)], wide_b[...])

        k = (t - 4 * PACE) // 2

        @pl.when((k >= 0) & (k < PIECES) & (t % 2 == 0))
        def _():
            trade(k).start()

        @pl.when(beat & (tick == 6))
        def _():
            for copy in loads_mid:
                copy.start()

        @pl.when(beat & (tick == 7))
        def _():
            for copy in loads_mid:
                copy.wait()

        @pl.when(beat & (tick >= 7) & (tick < 14))
        def _():
            g_ref[unit(1 + tick), :] = both(slab_a, wide_a, tick - 7)

        @pl.when(beat & (tick == 14))
        def _():
            g_ref[pl.ds(3 * DV + 384, DV - 384), :] = both(slab_a, wide_a, 7)[: DV - 384]

        @pl.when(beat & (tick == 15))
        def _():
            for copy in loads_in:
                copy.start()

        @pl.when(beat & (tick == 17))
        def _():
            for copy in loads_in:
                copy.wait()

        @pl.when(beat & (tick >= 17) & (tick < 29))
        def _():
            g_ref[unit(3 + tick), :] = both(slab_b, wide_a, tick - 17)

        return carry

    lax.fori_loop(0, n + 6 * LAG + 1, step, 0)

    for k in range(PIECES):
        trade(k).wait_send()
    for flow in range(2):
        p = z if flow == 0 else 3 - z
        mine = (whole + 1 - flow) // 2

        def drain(sem, count):
            part = land_ref.at[pl.ds(0, count * CHUNK)]
            pltpu.make_async_copy(part, part, sem).wait()

        @pl.when(p < 3)
        def _():
            drain(send_sem.at[flow], n)

        @pl.when(p > 0)
        def _():
            drain(far_sem.at[flow], n)

        @pl.when(p == 3)
        def _():
            drain(own_sem, n)
            drain(cross_sent, mine)

        drain(side_sem.at[flow], n - mine)
    got = full_ref.at[1 - x, pl.ds(whole * CHUNK, (2 * n - whole) * CHUNK)]
    pltpu.make_async_copy(got, got, near_sem).wait()


def chain_sum(
    small, hidden, cot, mixed, grad_branch, d1, d2, far_d1, far_d2, mid, far_mid, near, far, normed, far_normed
):
    T, D = mid.shape
    unit = 2 * CHUNK
    total = -(-(7 * DV + 2 * DK + 16) // unit) * unit
    chunks = total // CHUNK
    dma = pltpu.SemaphoreType.DMA
    return pl.pallas_call(
        functools.partial(chain_kernel, chunks // 2),
        out_shape=jax.ShapeDtypeStruct((2, total, D), BF16),
        in_specs=[pl.BlockSpec(memory_space=pl.ANY)] * 15,
        out_specs=pl.BlockSpec(memory_space=pl.ANY),
        scratch_shapes=[
            pltpu.VMEM((total, D), BF16), pltpu.VMEM((total, D), BF16), pltpu.VMEM((-(-DV // unit) * unit, D), BF16),
            pltpu.VMEM((2, T, D), BF16), pltpu.VMEM((T, D), BF16),
            pltpu.VMEM((2, T, 2 * DVP), BF16), pltpu.VMEM((2, T, 2 * DVP + 2 * DK), BF16),
            pltpu.VMEM((DVP, D), BF16), pltpu.VMEM((DVP, D), BF16),
            dma((15,)), dma((PIECES,)), dma((PIECES,)), dma((DV // CHUNK + 1,)), dma, dma((chunks,)), dma((chunks,)), dma((2,)), dma((2,)), dma((2,)),
            dma, dma,
        ],
        compiler_params=pltpu.CompilerParams(
            collective_id=0, has_side_effects=True, vmem_limit_bytes=63 * 2**20
        ),
        name="gradient_chains",
    )(
        small, hidden, cot, mixed, grad_branch, d1, d2, far_d1, far_d2, mid, far_mid, near, far, normed, far_normed,
    )


def finish_kernel(layout, full_ref, small_ref, whole_ref, *outs):
    row = layout[-1][0] + layout[-1][1]
    small_ref[...] = full_ref[0, row : row + 8, :].astype(F32) + full_ref[1, row : row + 8, :].astype(F32)
    x = lax.axis_index("seq") % 2
    whole = whole_ref.shape[0]
    whole_ref[...] = jnp.where(x == 0, full_ref[0, :whole, :], full_ref[1, :whole, :]).astype(F32)
    for (at, size, flip), out_ref in zip(layout, outs):
        for i in range(2):
            part = full_ref[i, at : at + size, :].astype(F32)
            if flip:
                out_ref[:, i * size : (i + 1) * size] = part.T
            else:
                out_ref[i * size : (i + 1) * size, :] = part


def finish(full, layout):
    D, tile = full.shape[2], 256
    lead = layout[0][0]
    specs = [pl.BlockSpec((8, tile), lambda i: (0, i)), pl.BlockSpec((lead, tile), lambda i: (0, i))]
    shapes = [jax.ShapeDtypeStruct((8, D), F32), jax.ShapeDtypeStruct((lead, D), F32)]
    for _, size, flip in layout:
        shapes.append(jax.ShapeDtypeStruct((D, 2 * size) if flip else (2 * size, D), F32))
        specs.append(
            pl.BlockSpec((tile, 2 * size), lambda i: (i, 0))
            if flip
            else pl.BlockSpec((2 * size, tile), lambda i: (0, i))
        )
    return pl.pallas_call(
        functools.partial(finish_kernel, layout),
        grid=(D // tile,),
        in_specs=[pl.BlockSpec((2, full.shape[1], tile), lambda i: (0, 0, i))],
        out_specs=specs,
        out_shape=shapes,
        compiler_params=pltpu.CompilerParams(vmem_limit_bytes=56 * 2**20),
        name="gradients_to_float32",
    )(full)


def offsets():
    return lax.broadcasted_iota(jnp.int32, (BLK, 1), 0).astype(F32)


def decay_row(logc, width, exponent):
    return jnp.exp(jnp.full((1, width), exponent, F32) * logc)


def decay_square(logc):
    row = lax.broadcasted_iota(jnp.int32, (BLK, BLK), 0)
    col = lax.broadcasted_iota(jnp.int32, (BLK, BLK), 1)
    lag = (row - col).astype(F32)
    return jnp.where(lag >= 0, jnp.exp(jnp.maximum(lag, 0.0) * logc), 0.0)


def turn(values, cosine, sine):
    a, b = values[:, : DK // 2], values[:, DK // 2 :]
    return jnp.concatenate([a * cosine - b * sine, b * cosine + a * sine], axis=1)


def rows(b):
    return pl.ds(b * BLK, BLK)


def fwd_state_kernel(nb, logc_ref, q_ref, k_ref, v_ref, cos_ref, sin_ref, qo_ref, ko_ref, s_ref):
    logc = logc_ref[pl.program_id(0)]
    o = offsets()
    to_end = jnp.exp((BLK - 1.0 - o) * logc)
    across = decay_row(logc, DVP, float(BLK))
    state = None
    for b in range(nb):
        cosine, sine = cos_ref[rows(b), :], sin_ref[rows(b), :]
        qo_ref[rows(b), :] = turn(q_ref[rows(b), :], cosine, sine).astype(BF16)
        key = (turn(k_ref[rows(b), :], cosine, sine) * (1.0 / math.sqrt(DK))).astype(BF16)
        ko_ref[rows(b), :] = key
        scaled = (key.astype(F32) * to_end).astype(BF16)
        new = contract(scaled, v_ref[rows(b), :], 0, 0)
        state = new if state is None else across * state + new
        s_ref[b] = state


def total_state(b, logc, s_in, s_ref):
    carried = s_in if b == 0 else decay_row(logc, DVP, float(b * BLK)) * s_in
    return carried if b == 0 else carried + s_ref[b - 1]


def group_stats(retained):
    real = lax.broadcasted_iota(jnp.int32, retained.shape, 1) < DV
    mean = jnp.sum(retained, axis=1, keepdims=True) * (1.0 / DV)
    centred = jnp.where(real, retained - mean, 0.0)
    var = jnp.sum(centred * centred, axis=1, keepdims=True) * (1.0 / DV)
    inverse = lax.rsqrt(var + 0.5)
    return centred * inverse, inverse


def fwd_out_kernel(
    nb, logc_ref, q_ref, k_ref, v_ref, s_ref, in_ref, gate_ref, gain_ref, mixed_ref, ret_ref
):
    logc = logc_ref[pl.program_id(0)]
    mask = decay_square(logc)
    into = jnp.exp((offsets() + 1.0) * logc)
    s_in = in_ref[...]
    for b in range(nb):
        query = q_ref[rows(b), :]
        scores = contract(query, k_ref[rows(b), :], 1, 1)
        weights = (scores * mask).astype(BF16)
        state = total_state(b, logc, s_in, s_ref).astype(BF16)
        scaled = (query.astype(F32) * into).astype(BF16)
        retained = contract(weights, v_ref[rows(b), :], 1, 0) + contract(scaled, state, 1, 0)
        ret_ref[rows(b), :] = retained
        ohat, _ = group_stats(retained)
        gate = gate_ref[rows(b), :]
        act = gate * jax.nn.sigmoid(gate)
        mixed_ref[rows(b), :] = (act * (ohat * gain_ref[...])).astype(BF16)


def bwd_mix_kernel(
    nb, logc_ref, dm_ref, ret_ref, gate_ref, gain_ref, q_ref, dg_ref, dr_ref, gg_ref, ds_ref
):
    logc = logc_ref[pl.program_id(0)]
    into = jnp.exp((offsets() + 1.0) * logc)
    gain = gain_ref[...]
    total = jnp.zeros((1, DVP), F32)
    state = jnp.zeros((DK, DVP), F32)
    for b in range(nb):
        dmixed = dm_ref[rows(b), :]
        gate = gate_ref[rows(b), :]
        ohat, inverse = group_stats(ret_ref[rows(b), :])
        sig = jax.nn.sigmoid(gate)
        dgrouped = dmixed * (gate * sig)
        dg_ref[rows(b), :] = (
            dmixed * (ohat * gain) * sig * (1.0 + gate * (1.0 - sig))
        ).astype(BF16)
        total = total + jnp.sum(dgrouped * ohat, axis=0, keepdims=True)
        e = dgrouped * gain
        mean = jnp.sum(e, axis=1, keepdims=True) * (1.0 / DV)
        cross = jnp.sum(e * ohat, axis=1, keepdims=True) * (1.0 / DV)
        real = lax.broadcasted_iota(jnp.int32, e.shape, 1) < DV
        dret = jnp.where(real, inverse * (e - mean - ohat * cross), 0.0).astype(BF16)
        dr_ref[rows(b), :] = dret
        scaled = (q_ref[rows(b), :].astype(F32) * into).astype(BF16)
        new = contract(scaled, dret, 0, 0)
        state = state + (new if b == 0 else decay_row(logc, DVP, float(b * BLK)) * new)
    gg_ref[...] = total
    ds_ref[...] = state


def bwd_ret_kernel(
    nb, logc_ref, q_ref, k_ref, v_ref, dr_ref, s_ref, in_ref, out_ref, cos_ref, sin_ref,
    dq_ref, dk_ref, dv_ref,
):
    logc = logc_ref[pl.program_id(0)]
    mask = decay_square(logc)
    o = offsets()
    into = jnp.exp((o + 1.0) * logc)
    to_end = jnp.exp((BLK - 1.0 - o) * logc)
    across = decay_row(logc, DVP, float(BLK))
    s_in = in_ref[...]
    later = out_ref[...]
    for b in reversed(range(nb)):
        query, key = q_ref[rows(b), :], k_ref[rows(b), :]
        value, dret = v_ref[rows(b), :], dr_ref[rows(b), :]
        weights = (contract(query, key, 1, 1) * mask).astype(BF16)
        dweights = (contract(dret, value, 1, 1) * mask).astype(BF16)
        state = total_state(b, logc, s_in, s_ref).astype(BF16)
        low = later.astype(BF16)
        dquery = contract(dweights, key, 1, 0) + contract(dret, state, 1, 1) * into
        dkey = contract(dweights, query, 0, 0) + contract(value, low, 1, 1) * to_end
        scaled = (key.astype(F32) * to_end).astype(BF16)
        dvalue = contract(weights, dret, 0, 0) + contract(scaled, low, 1, 0)
        cosine, sine = cos_ref[rows(b), :], sin_ref[rows(b), :]
        dq_ref[rows(b), :] = turn(dquery, cosine, -sine).astype(BF16)
        dk_ref[rows(b), :] = (turn(dkey, cosine, -sine) * (1.0 / math.sqrt(DK))).astype(BF16)
        dv_ref[rows(b), :] = dvalue.astype(BF16)
        if b > 0:
            qs = (query.astype(F32) * into).astype(BF16)
            later = across * later + contract(qs, dret, 0, 0)


def per_head(kernel, heads, T, ins, outs, name):
    nb = T // BLK

    def spec(kind):
        if kind == "smem":
            return pl.BlockSpec(memory_space=pltpu.SMEM)
        if kind == "rot":
            return pl.BlockSpec((T, DK // 2), lambda h: (0, 0))
        if kind == "key":
            return pl.BlockSpec((T, DK), lambda h: (0, h))
        if kind == "val":
            return pl.BlockSpec((T, DVP), lambda h: (0, h))
        if kind == "gain":
            return pl.BlockSpec((1, DVP), lambda h: (0, h))
        if kind == "state":
            return pl.BlockSpec((None, DK, DVP), lambda h: (h, 0, 0))
        if kind == "states":
            return pl.BlockSpec((nb, None, DK, DVP), lambda h: (0, h, 0, 0))
        raise ValueError(kind)

    def shape(kind, dtype):
        full = {
            "key": (T, heads * DK),
            "val": (T, heads * DVP),
            "gain": (1, heads * DVP),
            "state": (heads, DK, DVP),
            "states": (nb, heads, DK, DVP),
        }[kind]
        return jax.ShapeDtypeStruct(full, dtype)

    return pl.pallas_call(
        functools.partial(kernel, nb),
        grid=(heads,),
        in_specs=[spec(kind) for kind in ins],
        out_specs=[spec(kind) for kind, _ in outs],
        out_shape=[shape(kind, dtype) for kind, dtype in outs],
        compiler_params=pltpu.CompilerParams(vmem_limit_bytes=48 * 2**20),
        name=name,
    )


ROWS = 128


def own_block(value):
    h = lax.axis_index("head")
    y, c = h // 2, h % 2
    cols = value.shape[1] // 4
    part = [value[:, i * cols : (i + 1) * cols] for i in range(4)]
    return jnp.where(y == 0, jnp.where(c == 0, part[0], part[1]), jnp.where(c == 0, part[2], part[3]))


def reduce_scatter(scratch):
    keep, give, near, far, give_sem, near_sem, far_sent, far_sem = scratch
    h = lax.axis_index("head")
    y, c = h // 2, h % 2
    sibling, across = h + 1 - 2 * c, h + 2 - 4 * y
    cols = far.shape[1]

    def at(r):
        return pl.ds(pl.multiple_of(r * ROWS, ROWS), ROWS)

    def remote(src, dst, sent, got, to):
        return pltpu.make_async_remote_copy(
            src_ref=src, dst_ref=dst, send_sem=sent, recv_sem=got,
            device_id={"head": to}, device_id_type=MESH,
        )

    def to_sibling(r):
        slot = lax.rem(r, 2)
        return remote(give.at[slot], near.at[at(r)], give_sem.at[slot], near_sem.at[r], sibling)

    def spread(r, terms):
        slot = lax.rem(r, 2)

        @pl.when(r >= 2)
        def _():
            to_sibling(r).wait_send()

        part = [terms[:, i * cols : (i + 1) * cols] for i in range(4)]
        for i in range(2):
            place = slice(i * cols, (i + 1) * cols)
            keep[slot, :, place] = jnp.where(c == 0, part[2 * i], part[2 * i + 1])
            give[slot, :, place] = jnp.where(c == 0, part[2 * i + 1], part[2 * i]).astype(BF16)
        to_sibling(r).start()

    def collect(r):
        slot = lax.rem(r, 2)
        pltpu.make_async_copy(near.at[at(r)], near.at[at(r)], near_sem.at[r]).wait()
        chip = (keep[slot] + near[at(r), :].astype(F32)).astype(BF16)
        first, last = chip[:, :cols], chip[:, cols:]
        near[at(r), :cols] = jnp.where(y == 0, last, first)
        near[at(r), cols:] = jnp.where(y == 0, first, last)

    def pass_on(r):
        remote(near.at[at(r), pl.ds(0, cols)], far.at[at(r)], far_sent, far_sem.at[r], across).start()

    def gather(r):
        pltpu.make_async_copy(far.at[at(r)], far.at[at(r)], far_sem.at[r]).wait()
        return near[at(r), cols:].astype(F32) + far[at(r), :].astype(F32)

    def drain_near():
        for slot in range(2):
            to_sibling(slot).wait_send()

    def drain():
        drain_near()
        pltpu.make_async_copy(far, far, far_sent).wait()

    return spread, collect, pass_on, gather, drain_near, drain


def scatter_scratch(T, D):
    dma, nr = pltpu.SemaphoreType.DMA, T // ROWS
    return [
        pltpu.VMEM((2, ROWS, D // 2), F32), pltpu.VMEM((2, ROWS, D // 2), BF16),
        pltpu.VMEM((T, D // 2), BF16), pltpu.VMEM((T, D // 4), BF16),
        dma((2,)), dma((nr,)), dma, dma((nr,)),
    ]


def middle_general(mixed, all_tokens, all_cot, wo, w1, w2, w3, gain, heads):
    wo, w1, w2, w3 = [pad_rows(w, heads) for w in (wo, w1, w2, w3)]
    cols = all_tokens.shape[1] // lax.axis_size("head")
    own = lax.axis_index("head") * cols
    resid = all_tokens.astype(F32) + head_allreduce(jnp.dot(mixed, wo, preferred_element_type=F32))
    normal, inverse = row_stats(resid, 1e-05)
    normed = (normal * gain).astype(BF16)
    up_one, up_two = contract(normed, w1, 1, 1), contract(normed, w2, 1, 1)
    gelu_one, gelu_slope = gelu_parts(up_one)
    hidden = (gelu_one * up_two).astype(BF16)
    own_resid = lax.dynamic_slice_in_dim(resid, own, cols, axis=1)
    mlp_terms = jnp.dot(hidden, w3, preferred_element_type=F32)
    output = own_resid + head_reduce_scatter(mlp_terms)
    grad_hidden = contract(all_cot, w3, 1, 1)
    grad_one = (grad_hidden * up_two * gelu_slope).astype(BF16)
    grad_two = (grad_hidden * gelu_one).astype(BF16)
    grad = head_allreduce(
        jnp.dot(grad_one, w1, preferred_element_type=F32)
        + jnp.dot(grad_two, w2, preferred_element_type=F32)
    )
    gain_grad = jnp.sum(grad * normal, axis=0, keepdims=True)
    e = grad * gain
    resid_grad = all_cot.astype(F32) + inverse * (
        e
        - jnp.mean(e, axis=-1, keepdims=True)
        - normal * jnp.mean(e * normal, axis=-1, keepdims=True)
    )
    return (
        normed, hidden, grad_one, grad_two, output, None, resid_grad.astype(BF16),
        lax.dynamic_slice_in_dim(resid_grad, own, cols, axis=1),
        None,
        None,
        None,
        gain_grad,
    )


def middle_body(
    nr,
    parts,
    mixed_h, tok_h, cot_h, wo_h, w1_h, w2_h, w3_h, gain_ref,
    n2_h, hid_h, d1_h, d2_h, res_h, chip_h, db_h, dr_h, far2_h, far_d1_h, far_d2_h, mg_ref,
    mixed, tok, cot, wo, w1, w2, w3,
    keep, give, near, far, tot,
    s_n2, s_hid, s_d1, s_d2, s_res, s_db, s_dr,
    load_sem, mixed_sem, share_sem, shared_sem, hand_sem, acts_sem, give_sem, near_sem, far_sent, far_sem, tot_sent, tot_sem, out_sem,
    *scatter,
):
    h = lax.axis_index("head")
    y, c = h // 2, h % 2
    sibling, across = h + 1 - 2 * c, h + 2 - 4 * y
    D = tok.shape[1]
    half, cols = D // 2, D // 4

    s = lax.axis_index("seq")
    x = lax.rem(s, 2)
    partner = s + 1 - 2 * x
    U = w1.shape[0]
    real, room = w1_h.shape[0] // parts, U // parts
    loads = [
        pltpu.make_async_copy(tok_h, tok, load_sem.at[0]),
        pltpu.make_async_copy(cot_h, cot, load_sem.at[1]),
    ]
    weights = []
    for k, (src, dst) in enumerate([(wo_h, wo), (w1_h, w1), (w2_h, w2), (w3_h, w3)]):
        weights.append([
            pltpu.make_async_copy(
                src.at[pl.ds(i * real, real)], dst.at[pl.ds(i * room, real)], load_sem.at[2 + k * parts + i]
            )
            for i in range(parts)
        ])
    def at(r):
        return pl.ds(pl.multiple_of(r * ROWS, ROWS), ROWS)

    def fetch(r):
        slot = lax.rem(r, 2)
        return pltpu.make_async_copy(mixed_h.at[at(r)], mixed.at[slot], mixed_sem.at[slot])

    fetch(0).start()
    for load in weights[0]:
        load.start()
    fetch(1).start()
    for load in loads + weights[1] + weights[2] + weights[3]:
        load.start()
    for dst in (wo, w1, w2, w3):
        for i in range(parts):
            dst[i * room + real : (i + 1) * room, :] = jnp.zeros((room - real, D), BF16)
    barrier = pltpu.get_barrier_semaphore()
    for other in (sibling, across):
        pl.semaphore_signal(barrier, inc=1, device_id={"head": other}, device_id_type=MESH)
    pl.semaphore_signal(barrier, inc=1, device_id={"seq": partner}, device_id_type=MESH)
    pl.semaphore_wait(barrier, 3)
    mg_ref[...] = jnp.zeros_like(mg_ref)

    mine = pl.ds(pl.multiple_of(c * half, 128), half)
    theirs = pl.ds(pl.multiple_of((1 - x) * room, 128), room)

    def share(k, r):
        slot = lax.rem(r, 2)
        if k == 0:
            src, dst, got = s_n2.at[slot, :, mine], far2_h.at[at(r), mine], share_sem.at[r]
        else:
            stage, far_h = ((s_d1, far_d1_h), (s_d2, far_d2_h))[k - 1]
            src, dst, got = stage.at[slot, :, theirs], far_h.at[at(r)], acts_sem.at[k - 1]
        return pltpu.make_async_remote_copy(
            src_ref=src, dst_ref=dst, send_sem=shared_sem.at[k, slot], recv_sem=got,
            device_id={"seq": partner}, device_id_type=MESH,
        )

    def hand(r):
        here = far2_h.at[at(r), mine]
        return pltpu.make_async_remote_copy(
            src_ref=here, dst_ref=here, send_sem=hand_sem.at[0], recv_sem=hand_sem.at[1],
            device_id={"head": sibling}, device_id_type=MESH,
        )

    for load in weights[0]:
        load.wait()

    def remote(src, dst, sent, got, to):
        return pltpu.make_async_remote_copy(
            src_ref=src, dst_ref=dst, send_sem=sent, recv_sem=got,
            device_id={"head": to}, device_id_type=MESH,
        )

    def first(a, r, terms):
        slot = lax.rem(r, 2)

        @pl.when(r >= 2)
        def _():
            pltpu.make_async_copy(give.at[a, slot], give.at[a, slot], give_sem.at[a, slot]).wait()

        lo, hi = terms[:, :half], terms[:, half:]
        keep[a] = jnp.where(c == 0, lo, hi)
        give[a, slot] = jnp.where(c == 0, hi, lo).astype(BF16)
        remote(give.at[a, slot], near.at[a, at(r)], give_sem.at[a, slot], near_sem.at[a, r], sibling).start()

    def second(a, r):
        here = near.at[a, at(r)]
        pltpu.make_async_copy(here, here, near_sem.at[a, r]).wait()
        near[a, at(r)] = (keep[a] + near[a, at(r)].astype(F32)).astype(BF16)
        remote(here, far.at[a, at(r)], far_sent.at[a], far_sem.at[a, r], across).start()

    def third(a, r):
        here = far.at[a, at(r)]
        pltpu.make_async_copy(here, here, far_sem.at[a, r]).wait()
        tot[a, c, at(r)] = (near[a, at(r)].astype(F32) + far[a, at(r)].astype(F32)).astype(BF16)
        here = tot.at[a, c, at(r)]
        remote(here, here, tot_sent.at[a], tot_sem.at[a, r], sibling).start()

    def joined(a, r):
        return jnp.concatenate([tot[a, 0, at(r)], tot[a, 1, at(r)]], axis=1).astype(F32)

    def arrive(a, r):
        here = tot.at[a, 1 - c, at(r)]
        pltpu.make_async_copy(here, here, tot_sem.at[a, r]).wait()

    def put(k, r, stage, dst, value, shared=None):
        slot = lax.rem(r, 2)
        copy = pltpu.make_async_copy(stage.at[slot], dst.at[at(r)], out_sem.at[k, slot])

        @pl.when(r >= 2)
        def _():
            copy.wait()
            if shared is not None:
                share(shared, r).wait_send()

        stage[slot] = value
        copy.start()
        if shared is not None:
            share(shared, r).start()

    spread, collect, _, _, drain_near, _ = reduce_scatter(scatter)

    def step(t, carry):
        for a, late in ((0, 1), (1, 4)):
            r = t - late

            @pl.when((r >= 0) & (r < nr))
            def _():
                second(a, r)

        r = t - 4

        @pl.when((r >= 0) & (r < nr))
        def _():
            collect(r)

        for a, late in ((0, 2), (1, 5)):
            r = t - late

            @pl.when((r >= 0) & (r < nr))
            def _():
                third(a, r)

        @pl.when(t < nr)
        def _():
            fetch(t).wait()
            first(0, t, jnp.dot(mixed[lax.rem(t, 2)], wo[...], preferred_element_type=F32))

        @pl.when(t + 2 < nr)
        def _():
            fetch(t + 2).start()

        r = t - 3

        @pl.when(r == 0)
        def _():
            for load in loads + weights[1] + weights[2] + weights[3]:
                load.wait()

        @pl.when((r >= 0) & (r < nr))
        def _():
            arrive(0, r)
            resid = tok[at(r), :].astype(F32) + joined(0, r)
            put(0, r, s_res, res_h, own_block(resid))
            normal, _ = row_stats(resid, 1e-05)
            normed = (normal * gain_ref[...]).astype(BF16)
            put(1, r, s_n2, n2_h, normed, 0)
            up_one, up_two = contract(normed, w1[...], 1, 1), contract(normed, w2[...], 1, 1)
            grad_hidden = contract(cot[at(r), :], w3[...], 1, 1)
            gelu_one, gelu_slope = gelu_parts(up_one)
            hidden = (gelu_one * up_two).astype(BF16)
            grad_one = (grad_hidden * up_two * gelu_slope).astype(BF16)
            grad_two = (grad_hidden * gelu_one).astype(BF16)
            terms = jnp.dot(grad_one, w1[...], preferred_element_type=F32)
            first(1, r, terms + jnp.dot(grad_two, w2[...], preferred_element_type=F32))
            put(2, r, s_hid, hid_h, hidden)
            put(3, r, s_d1, d1_h, grad_one, 1)
            put(4, r, s_d2, d2_h, grad_two, 2)
            spread(r, jnp.dot(hidden, w3[...], preferred_element_type=F32))

        g = t - 6

        @pl.when(g >= 0)
        def _():
            arrive(1, g)
            normal, inverse = row_stats(tok[at(g), :].astype(F32) + joined(0, g), 1e-05)
            grad = joined(1, g)
            mg_ref[...] += jnp.sum(grad * normal, axis=0, keepdims=True)
            e = grad * gain_ref[...]
            resid_grad = cot[at(g), :].astype(F32) + inverse * (
                e
                - jnp.mean(e, axis=-1, keepdims=True)
                - normal * jnp.mean(e * normal, axis=-1, keepdims=True)
            )
            put(5, g, s_db, db_h, resid_grad.astype(BF16))
            put(6, g, s_dr, dr_h, own_block(resid_grad))

        r = t - 5

        @pl.when((r >= 0) & (r < nr))
        def _():
            here = far2_h.at[at(r), mine]
            pltpu.make_async_copy(here, here, share_sem.at[r]).wait()
            hand(r).start()

        return carry

    lax.fori_loop(0, nr + 6, step, 0)

    other = far2_h.at[:, pl.ds(pl.multiple_of((1 - c) * half, 128), half)]
    pltpu.make_async_copy(other, other, hand_sem.at[0]).wait()
    pltpu.make_async_copy(other, other, hand_sem.at[1]).wait()
    for k in range(3):
        for slot in range(2):
            share(k, slot).wait_send()
    pltpu.make_async_copy(far_d1_h, far_d1_h, acts_sem.at[0]).wait()
    pltpu.make_async_copy(far_d2_h, far_d2_h, acts_sem.at[1]).wait()
    for a in range(2):
        for slot in range(2):
            pltpu.make_async_copy(give.at[a, slot], give.at[a, slot], give_sem.at[a, slot]).wait()
        pltpu.make_async_copy(far.at[a], far.at[a], far_sent.at[a]).wait()
        pltpu.make_async_copy(tot.at[a, 0], tot.at[a, 0], tot_sent.at[a]).wait()
    drain_near()
    chips = pltpu.make_async_copy(scatter[2], chip_h, scatter[6])
    chips.start()
    chips.wait()
    for k, stage in enumerate([s_res, s_n2, s_hid, s_d1, s_d2, s_db, s_dr]):
        for slot in range(2):
            pltpu.make_async_copy(stage.at[slot], stage.at[slot], out_sem.at[k, slot]).wait()


def middle_kernel(mixed, all_tokens, all_cot, wo, w1, w2, w3, gain, heads):
    T, D = all_tokens.shape
    U, half, cols, nr = mixed.shape[1], D // 2, D // 4, T // ROWS
    low, wide = functools.partial(jax.ShapeDtypeStruct, dtype=BF16), functools.partial(
        jax.ShapeDtypeStruct, dtype=F32
    )
    anywhere, vmem = pl.BlockSpec(memory_space=pl.ANY), pl.BlockSpec(memory_space=pltpu.VMEM)
    dma = pltpu.SemaphoreType.DMA
    macs = T * U * D * 7
    return pl.pallas_call(
        functools.partial(middle_body, nr, heads),
        out_shape=[
            low((T, D)), low((T, U)), low((T, U)), low((T, U)), wide((T, cols)), low((T, half)),
            low((T, D)), wide((T, cols)), low((T, D)), low((T, U // heads)), low((T, U // heads)),
            wide((1, D)),
        ],
        in_specs=[anywhere] * 7 + [vmem],
        out_specs=[anywhere] * 11 + [vmem],
        scratch_shapes=[
            pltpu.VMEM((2, ROWS, U), BF16), pltpu.VMEM((T, D), BF16), pltpu.VMEM((T, D), BF16),
            pltpu.VMEM((U, D), BF16), pltpu.VMEM((U, D), BF16), pltpu.VMEM((U, D), BF16),
            pltpu.VMEM((U, D), BF16),
            pltpu.VMEM((2, ROWS, half), F32), pltpu.VMEM((2, 2, ROWS, half), BF16),
            pltpu.VMEM((2, T, half), BF16), pltpu.VMEM((2, T, half), BF16),
            pltpu.VMEM((2, 2, T, half), BF16),
            pltpu.VMEM((2, ROWS, D), BF16), pltpu.VMEM((2, ROWS, U), BF16),
            pltpu.VMEM((2, ROWS, U), BF16), pltpu.VMEM((2, ROWS, U), BF16),
            pltpu.VMEM((2, ROWS, cols), F32), pltpu.VMEM((2, ROWS, D), BF16),
            pltpu.VMEM((2, ROWS, cols), F32),
            dma((2 + 4 * heads,)), dma((2,)), dma((nr,)), dma((3, 2)), dma((2,)), dma((2,)), dma((2, 2)), dma((2, nr)), dma((2,)), dma((2, nr)), dma((2,)), dma((2, nr)),
            dma((7, 2)),
        ] + scatter_scratch(T, D),
        compiler_params=pltpu.CompilerParams(
            collective_id=1, has_side_effects=True, vmem_limit_bytes=63 * 2**20
        ),
        cost_estimate=pl.CostEstimate(
            flops=2 * macs, bytes_accessed=50 * 2**20, transcendentals=2 * T * U
        ),
        name="mixed_to_dbranch",
    )(mixed, all_tokens, all_cot, wo, w1, w2, w3, gain)


def carry_state(reverse, logc_ref, T, own, total, bufs, sems):
    low, side, into, out = bufs
    low_sem, side_sem, into_sem, out_sem = sems
    s = lax.axis_index("seq")
    z, x = s // 2, s % 2
    partner = s + 1 - 2 * x
    p = 3 - z if reverse else z
    ahead = s - 2 if reverse else s + 2
    first = (x == 1) if reverse else (x == 0)
    parts = 4
    size = DK // parts

    def remote(src, dst, sent, got, to):
        return pltpu.make_async_remote_copy(
            src_ref=src, dst_ref=dst, send_sem=sent, recv_sem=got,
            device_id={"seq": to}, device_id_type=MESH,
        )

    def part(i):
        return pl.ds(i * size, size)

    def trade(k, i):
        head = 1 - x if k == 0 else x
        return remote(low.at[head, part(i)], side.at[head, part(i)], low_sem.at[k, i], side_sem.at[k, i], partner)

    def forward(head, k, i):
        return remote(out.at[head, part(i)], into.at[head, part(i)], out_sem.at[k, i], into_sem.at[k, i], ahead)

    def factor(h, width=DVP):
        return jnp.exp(jnp.full((1, width), float(T), F32) * logc_ref[h])

    def start():
        low[...] = own[...].astype(BF16)
        for k in range(2):
            for i in range(parts):
                trade(k, i).start()

    def finish():
        for k in range(2):
            head = x if k == 0 else 1 - x
            f = factor(head)
            for i in range(parts):
                here = side.at[head, part(i)]
                pltpu.make_async_copy(here, here, side_sem.at[k, i]).wait()
                mine, others = low[head, part(i)].astype(F32), side[head, part(i)].astype(F32)
                early = jnp.where(first, mine, others)
                pair = f * early + jnp.where(first, others, mine)

                @pl.when(p == 0)
                def _():
                    out[head, part(i)] = pair.astype(BF16)
                    into[head, part(i)] = jnp.zeros((size, DVP), BF16)

                @pl.when(p > 0)
                def _():
                    here = into.at[head, part(i)]
                    pltpu.make_async_copy(here, here, into_sem.at[k, i]).wait()
                    out[head, part(i)] = (pair + f * f * into[head, part(i)].astype(F32)).astype(BF16)

                @pl.when(p < 3)
                def _():
                    forward(head, k, i).start()

                before = into[head, part(i)].astype(F32)
                total[head, part(i)] = jnp.where(first, before, f * before + early)

        for k in range(2):
            for i in range(parts):
                trade(k, i).wait_send()

                @pl.when(p < 3)
                def _():
                    forward(x if k == 0 else 1 - x, k, i).wait_send()

    return start, finish


def carry_scratch():
    dma = pltpu.SemaphoreType.DMA
    state = pltpu.VMEM((2, DK, DVP), BF16)
    return [state] * 4 + [dma((2, 4))] * 4


def greet(head_others, seq_partner):
    s = lax.axis_index("seq")
    z = s // 2
    barrier = pltpu.get_barrier_semaphore()
    for other in head_others:
        pl.semaphore_signal(barrier, inc=1, device_id={"head": other}, device_id_type=MESH)
    pl.semaphore_signal(barrier, inc=1, device_id={"seq": seq_partner}, device_id_type=MESH)

    @pl.when(z > 0)
    def _():
        pl.semaphore_signal(barrier, inc=1, device_id={"seq": s - 2}, device_id_type=MESH)

    @pl.when(z < 3)
    def _():
        pl.semaphore_signal(barrier, inc=1, device_id={"seq": s + 2}, device_id_type=MESH)

    pl.semaphore_wait(barrier, len(head_others) + jnp.where((z > 0) & (z < 3), 3, 2))


def front_body(
    nr, heads,
    logc_ref, tok_h, cot_h, gains_ref, wq_h, wk_h, wv_h, wg_h, cos_ref, sin_ref, gg_ref,
    all_h, cot_all_h, n1_h, far_h, q_h, k_h, v_h, gate_h, ret_h, mixed_h, states_h, in_h, full_ref,
    rows_v, wq, wk, wv, wg, q_v, k_v, v_v, gate_v, ret_v, mixed_v, states, state, s_in, s_n1,
    load_sem, y_sem, c_sem, d_sem, sent_sem, cot_sem, cot_sent, gain_sem, gain_sent, share_sem, shared_sem,
    hand_sem, out_sem, mix_sem,
    *carry,
):
    h = lax.axis_index("head")
    y, c = h // 2, h % 2
    sibling, across = h + 1 - 2 * c, h + 2 - 4 * y
    s = lax.axis_index("seq")
    partner = s + 1 - 2 * (s % 2)
    T, D = rows_v.shape
    half, cols = D // 2, D // 4
    real = wv_h.shape[0] // heads
    per_block = BLK // ROWS

    def at(r):
        return pl.ds(pl.multiple_of(r * ROWS, ROWS), ROWS)

    def block(i):
        return pl.ds(pl.multiple_of(i * cols, 128), cols)

    def remote(src, dst, sent, got, **to):
        return pltpu.make_async_remote_copy(
            src_ref=src, dst_ref=dst, send_sem=sent, recv_sem=got, device_id=to, device_id_type=MESH,
        )

    def landed(ref, sem):
        pltpu.make_async_copy(ref, ref, sem).wait()

    greet((sibling, across), partner)

    def to_across(r):
        return remote(tok_h.at[at(r)], rows_v.at[at(r), block(h)], sent_sem.at[0], y_sem.at[r], head=across)

    def to_sibling(r):
        return remote(tok_h.at[at(r)], rows_v.at[at(r), block(h)], sent_sem.at[1], c_sem.at[r], head=sibling)

    gain_own = gains_ref
    gain_y = remote(gain_own, full_ref.at[:, block(h)], gain_sent.at[0], gain_sem.at[0], head=across)
    gain_c = remote(gain_own, full_ref.at[:, block(h)], gain_sent.at[1], gain_sem.at[1], head=sibling)
    gain_d = remote(
        full_ref.at[:, block(across)], full_ref.at[:, block(across)], gain_sent.at[2], gain_sem.at[2], head=sibling
    )
    gain_y.start()
    gain_c.start()
    own_tokens = pltpu.make_async_copy(tok_h, rows_v.at[:, block(h)], load_sem.at[0])
    own_tokens.start()
    for r in range(nr):
        to_across(r).start()
        to_sibling(r).start()
    loads = [
        pltpu.make_async_copy(wq_h, wq, load_sem.at[1]), pltpu.make_async_copy(wk_h, wk, load_sem.at[2])
    ]
    for k, (src, dst) in enumerate([(wv_h, wv), (wg_h, wg)]):
        for i in range(heads):
            loads.append(
                pltpu.make_async_copy(
                    src.at[pl.ds(i * real, real)], dst.at[pl.ds(i * DVP, real)], load_sem.at[3 + k * heads + i]
                )
            )
    for load in loads:
        load.start()
    own_cot = pltpu.make_async_copy(cot_h, cot_all_h.at[:, block(h)], load_sem.at[3 + 2 * heads])
    own_cot.start()
    cot_y = remote(cot_h, cot_all_h.at[:, block(h)], cot_sent.at[0], cot_sem.at[0], head=across)
    cot_c = remote(cot_h, cot_all_h.at[:, block(h)], cot_sent.at[1], cot_sem.at[1], head=sibling)
    far_block = cot_all_h.at[:, block(across)]
    cot_d = remote(far_block, far_block, cot_sent.at[2], cot_sem.at[2], head=sibling)
    for dst in (wv, wg):
        for i in range(heads):
            dst[i * DVP + real : (i + 1) * DVP, :] = jnp.zeros((DVP - real, D), BF16)
    full_ref[:, block(h)] = gains_ref[...]
    state[...] = jnp.zeros_like(state)
    gain_y.wait_recv()
    gain_d.start()
    gain_c.wait_recv()
    gain_d.wait_recv()
    own_tokens.wait()

    mine = pl.ds(pl.multiple_of(c * half, 128), half)

    def share(r):
        slot = lax.rem(r, 2)
        return remote(
            s_n1.at[slot, :, mine], far_h.at[at(r), mine], shared_sem.at[slot], share_sem.at[r], seq=partner
        )

    def hand(r):
        here = far_h.at[at(r), mine]
        return remote(here, here, hand_sem.at[0], hand_sem.at[1], head=sibling)

    def keep(r):
        slot = lax.rem(r, 2)
        return pltpu.make_async_copy(s_n1.at[slot], n1_h.at[at(r)], out_sem.at[slot])

    def step(t, carried):
        @pl.when(t < nr)
        def _():
            here = rows_v.at[at(t), block(across)]
            landed(here, y_sem.at[t])
            remote(here, here, sent_sem.at[2], d_sem.at[t], head=sibling).start()

        @pl.when(t == nr - 2)
        def _():
            cot_y.start()
            cot_c.start()

        r = t - 1

        @pl.when(r == 0)
        def _():
            for load in loads:
                load.wait()

        @pl.when((r >= 0) & (r < nr))
        def _():
            slot = lax.rem(r, 2)
            landed(rows_v.at[at(r), block(sibling)], c_sem.at[r])
            diag = lax.rem(sibling + 2, 4)
            landed(rows_v.at[at(r), block(diag)], d_sem.at[r])
            normal, _ = row_stats(rows_v[at(r), :].astype(F32), 1e-05)
            normed = (normal * full_ref[0:1, :]).astype(BF16)

            @pl.when(r >= 2)
            def _():
                keep(r).wait()
                share(r).wait_send()

            s_n1[slot] = normed
            keep(r).start()
            share(r).start()
            query = jnp.dot(normed, wq[...], preferred_element_type=F32)
            key = jnp.dot(normed, wk[...], preferred_element_type=F32)
            value = contract(normed, wv[...], 1, 1).astype(BF16)
            v_v[at(r), :] = value
            gate_v[at(r), :] = contract(normed, wg[...], 1, 1)
            cosine, sine = cos_ref[at(r), :], sin_ref[at(r), :]
            o = lax.broadcasted_iota(jnp.int32, (ROWS, 1), 0).astype(F32)
            for i in range(heads):
                logc = logc_ref[i]
                keys = slice(i * DK, (i + 1) * DK)
                q_v[at(r), keys] = turn(query[:, keys], cosine, sine).astype(BF16)
                low = (turn(key[:, keys], cosine, sine) * (1.0 / math.sqrt(DK))).astype(BF16)
                k_v[at(r), keys] = low
                scaled = (low.astype(F32) * jnp.exp((ROWS - 1.0 - o) * logc)).astype(BF16)
                new = contract(scaled, value[:, i * DVP : (i + 1) * DVP], 0, 0)
                state[i] = decay_row(logc, DVP, float(ROWS)) * state[i] + new

            @pl.when(lax.rem(r, per_block) == per_block - 1)
            def _():
                states[r // per_block] = state[...]

        g = t - 3

        @pl.when(g >= 0)
        def _():
            here = far_h.at[at(g), mine]
            landed(here, share_sem.at[g])
            hand(g).start()

        return carried

    begin, end = carry_state(False, logc_ref, T, state, s_in, carry[:4], carry[4:])
    lax.fori_loop(0, nr + 1, step, 0)
    begin()
    outs = [
        pltpu.make_async_copy(src, dst, out_sem.at[2 + i])
        for i, (src, dst) in enumerate(
            [(rows_v, all_h), (q_v, q_h), (k_v, k_h), (v_v, v_h), (gate_v, gate_h), (states, states_h)]
        )
    ]
    for copy in outs:
        copy.start()
    cot_y.wait_recv()
    cot_d.start()

    nb = T // BLK
    for i in range(heads):
        mask = decay_square(logc_ref[i])
        for b in range(nb):
            keys, vals = slice(i * DK, (i + 1) * DK), slice(i * DVP, (i + 1) * DVP)
            scores = contract(q_v[rows(b), keys], k_v[rows(b), keys], 1, 1)
            weights = (scores * mask).astype(BF16)
            ret_v[rows(b), vals] = jnp.dot(weights, v_v[rows(b), vals], preferred_element_type=F32)
    end()
    keep_in = pltpu.make_async_copy(s_in, in_h, out_sem.at[8])
    keep_in.start()
    tail = []
    for i in range(heads):
        logc = logc_ref[i]
        into = jnp.exp((offsets() + 1.0) * logc)
        for b in range(nb):
            keys, vals = slice(i * DK, (i + 1) * DK), slice(i * DVP, (i + 1) * DVP)
            total = s_in[i] if b == 0 else decay_row(logc, DVP, float(b * BLK)) * s_in[i] + states[b - 1, i]
            scaled = (q_v[rows(b), keys].astype(F32) * into).astype(BF16)
            retained = ret_v[rows(b), vals] + jnp.dot(
                scaled, total.astype(BF16), preferred_element_type=F32
            )
            ret_v[rows(b), vals] = retained
            ohat, _ = group_stats(retained)
            gate = gate_v[rows(b), vals]
            act = gate * jax.nn.sigmoid(gate)
            mixed_v[rows(b), vals] = (act * (ohat * gg_ref[:, vals])).astype(BF16)
            for k, (src, dst) in enumerate([(ret_v, ret_h), (mixed_v, mixed_h)]):
                copy = pltpu.make_async_copy(
                    src.at[rows(b), vals], dst.at[rows(b), vals], mix_sem.at[k, i * nb + b]
                )
                copy.start()
                tail.append(copy)

    for copy in outs + tail + [keep_in, own_cot]:
        copy.wait()
    lax.fori_loop(nr + 1, nr + 3, step, 0)
    for slot in range(2):
        keep(slot).wait()
        share(slot).wait_send()
    other = far_h.at[:, pl.ds(pl.multiple_of((1 - c) * half, 128), half)]
    landed(other, hand_sem.at[0])
    landed(other, hand_sem.at[1])
    own_columns = rows_v.at[:, block(h)]
    for k in range(3):
        landed(own_columns, sent_sem.at[k])
    gain_y.wait_send()
    gain_c.wait_send()
    gain_d.wait_send()
    cot_c.wait_recv()
    cot_d.wait_recv()
    cot_y.wait_send()
    cot_c.wait_send()
    cot_d.wait_send()


def front_kernel(
    logc, tokens, cotangent, gains, w_query, w_key, wv, wg, cosine, sine, group_gain, heads
):
    T, cols = tokens.shape
    D, nr, nb = 4 * cols, T // ROWS, T // BLK
    keys, vals = heads * DK, heads * DVP
    low = functools.partial(jax.ShapeDtypeStruct, dtype=BF16)
    wide = functools.partial(jax.ShapeDtypeStruct, dtype=F32)
    anywhere, vmem = pl.BlockSpec(memory_space=pl.ANY), pl.BlockSpec(memory_space=pltpu.VMEM)
    dma = pltpu.SemaphoreType.DMA
    return pl.pallas_call(
        functools.partial(front_body, nr, heads),
        out_shape=[
            low((T, D)), low((T, D)), low((T, D)), low((T, D)), low((T, keys)), low((T, keys)),
            low((T, vals)), wide((T, vals)), wide((T, vals)), low((T, vals)),
            wide((nb, heads, DK, DVP)), wide((heads, DK, DVP)), wide((8, D)),
        ],
        in_specs=[pl.BlockSpec(memory_space=pltpu.SMEM)] + [anywhere] * 2 + [vmem] + [anywhere] * 4 + [vmem] * 3,
        out_specs=[anywhere] * 12 + [vmem],
        scratch_shapes=[
            pltpu.VMEM((T, D), BF16), pltpu.VMEM((D, keys), BF16), pltpu.VMEM((D, keys), BF16),
            pltpu.VMEM((vals, D), BF16), pltpu.VMEM((vals, D), BF16),
            pltpu.VMEM((T, keys), BF16), pltpu.VMEM((T, keys), BF16), pltpu.VMEM((T, vals), BF16),
            pltpu.VMEM((T, vals), F32), pltpu.VMEM((T, vals), F32), pltpu.VMEM((T, vals), BF16),
            pltpu.VMEM((nb, heads, DK, DVP), F32), pltpu.VMEM((heads, DK, DVP), F32),
            pltpu.VMEM((heads, DK, DVP), F32), pltpu.VMEM((2, ROWS, D), BF16),
            dma((4 + 2 * heads,)), dma((nr,)), dma((nr,)), dma((nr,)), dma((3,)), dma((3,)), dma((3,)),
            dma((3,)), dma((3,)), dma((nr,)), dma((2,)), dma((2,)), dma((9,)), dma((2, heads * nb)),
        ] + carry_scratch(),
        compiler_params=pltpu.CompilerParams(
            collective_id=2, has_side_effects=True, vmem_limit_bytes=60 * 2**20
        ),
        cost_estimate=pl.CostEstimate(
            flops=2 * T * D * 2 * (keys + vals), bytes_accessed=60 * 2**20, transcendentals=T * vals
        ),
        name="tokens_to_mixed",
    )(logc, tokens, cotangent, gains, w_query, w_key, wv, wg, cosine, sine, group_gain)


def back_body(
    nr, heads,
    logc_ref, db_h, wo_h, ret_h, gate_h, gg_ref, q_h, k_h, v_h, states_h, in_h, cos_ref, sin_ref,
    wq_h, wk_h, wv_h, wg_h, tok_h, gain_ref, dr_h, chip_h,
    near_h, far_h, sums_h, gg_grad_ref, gt_h, ng_ref,
    rows_v, big, wq, wk, wg, ret, gate, q_v, k_v, v_v, states, s_in, dr_v,
    dg, dret, dq, dk, dv, ds, later, s_gt,
    side, side_give, side_far,
    load_sem, late_sem, act_sem, act_sent, sums_sem, near_sem, gt_sem, side_sem, side_sent, side_got, side_gone,
    *rest,
):
    carry, scatter = rest[:8], rest[8:]
    h = lax.axis_index("head")
    y, c = h // 2, h % 2
    sibling, across = h + 1 - 2 * c, h + 2 - 4 * y
    s = lax.axis_index("seq")
    x = s % 2
    partner = s + 1 - 2 * x
    T, D = rows_v.shape
    real = wo_h.shape[0] // heads
    nb = T // BLK

    def at(r):
        return pl.ds(pl.multiple_of(r * ROWS, ROWS), ROWS)

    def padded(src, dst, sems, k):
        return [
            pltpu.make_async_copy(src.at[pl.ds(i * real, real)], dst.at[pl.ds(i * DVP, real)], sems.at[k + i])
            for i in range(heads)
        ]

    early = [pltpu.make_async_copy(db_h, rows_v, load_sem.at[0])] + padded(wo_h, big, load_sem, 1)
    pairs = [(ret_h, ret), (gate_h, gate), (q_h, q_v), (k_h, k_v), (v_h, v_v), (states_h, states), (in_h, s_in)]
    pairs += [(wq_h, wq), (wk_h, wk), (dr_h, dr_v)]
    others = [
        pltpu.make_async_copy(src, dst, load_sem.at[1 + heads + i]) for i, (src, dst) in enumerate(pairs)
    ] + padded(wg_h, wg, load_sem, 1 + heads + len(pairs))
    for load in early + others:
        load.start()
    for dst in (big, wg):
        for i in range(heads):
            dst[i * DVP + real : (i + 1) * DVP, :] = jnp.zeros((DVP - real, D), BF16)
    greet((sibling, across), partner)
    mlp = pltpu.make_async_remote_copy(
        src_ref=chip_h.at[:, pl.ds(0, D // 4)], dst_ref=sums_h, send_sem=sums_sem.at[0], recv_sem=sums_sem.at[1],
        device_id={"head": across}, device_id_type=MESH,
    )
    mlp.start()
    for load in early + others[:3]:
        load.wait()

    def send_half(k, value, place, width):
        stay = pltpu.make_async_copy(
            value.at[:, pl.ds(pl.multiple_of(x * width, 128), width)], near_h.at[:, pl.ds(place, width)],
            near_sem.at[k],
        )
        go = pltpu.make_async_remote_copy(
            src_ref=value.at[:, pl.ds(pl.multiple_of((1 - x) * width, 128), width)],
            dst_ref=far_h.at[:, pl.ds(place, width)], send_sem=act_sent.at[k], recv_sem=act_sem.at[k],
            device_id={"seq": partner}, device_id_type=MESH,
        )
        stay.start()
        go.start()
        return stay, go

    for i in range(heads):
        logc = logc_ref[i]
        into = jnp.exp((offsets() + 1.0) * logc)
        keys, vals = slice(i * DK, (i + 1) * DK), slice(i * DVP, (i + 1) * DVP)
        gain = gg_ref[:, vals]
        for b in range(nb):
            dmixed = contract(rows_v[rows(b), :], big[vals, :], 1, 1)
            g = gate[rows(b), vals]
            ohat, inverse = group_stats(ret[rows(b), vals])
            sig = jax.nn.sigmoid(g)
            dgrouped = dmixed * (g * sig)
            dg[rows(b), vals] = (dmixed * (ohat * gain) * sig * (1.0 + g * (1.0 - sig))).astype(BF16)
            total = jnp.sum(dgrouped * ohat, axis=0, keepdims=True)
            e = dgrouped * gain
            mean = jnp.sum(e, axis=1, keepdims=True) * (1.0 / DV)
            cross = jnp.sum(e * ohat, axis=1, keepdims=True) * (1.0 / DV)
            inside = lax.broadcasted_iota(jnp.int32, e.shape, 1) < DV
            low = jnp.where(inside, inverse * (e - mean - ohat * cross), 0.0).astype(BF16)
            dret[rows(b), vals] = low
            scaled = (q_v[rows(b), keys].astype(F32) * into).astype(BF16)
            new = contract(scaled, low, 0, 0)
            if b == 0:
                gg_grad_ref[:, vals] = total
                ds[i] = new
            else:
                gg_grad_ref[:, vals] += total
                ds[i] += decay_row(logc, DVP, float(b * BLK)) * new
    begin, end = carry_state(True, logc_ref, T, ds, later, carry[:4], carry[4:])
    begin()
    halves = []
    tokens_in = pltpu.make_async_copy(tok_h, rows_v, late_sem.at[0])
    values_in = padded(wv_h, big, late_sem, 1)
    tokens_in.start()
    for load in values_in:
        load.start()
    for load in others[3:]:
        load.wait()

    for i in range(heads):
        logc = logc_ref[i]
        mask = decay_square(logc)
        into = jnp.exp((offsets() + 1.0) * logc)
        keys, vals = slice(i * DK, (i + 1) * DK), slice(i * DVP, (i + 1) * DVP)
        for b in range(nb):
            query, key = q_v[rows(b), keys], k_v[rows(b), keys]
            value, low = v_v[rows(b), vals], dret[rows(b), vals]
            weights = (contract(query, key, 1, 1) * mask).astype(BF16)
            dweights = (contract(low, value, 1, 1) * mask).astype(BF16)
            state = s_in[i] if b == 0 else decay_row(logc, DVP, float(b * BLK)) * s_in[i] + states[b - 1, i]
            dquery = jnp.dot(dweights, key, preferred_element_type=F32)
            dquery = dquery + contract(low, state.astype(BF16), 1, 1) * into
            dq[rows(b), keys] = turn(dquery, cos_ref[rows(b), :], -sin_ref[rows(b), :]).astype(BF16)
            gate[rows(b), keys] = contract(dweights, query, 0, 0)
            ret[rows(b), vals] = contract(weights, low, 0, 0)
    halves.append(send_half(0, dg, 0, DVP))
    halves.append(send_half(1, dq, 2 * DVP, DK))
    end()
    for i in range(heads):
        logc = logc_ref[i]
        o = offsets()
        into, to_end = jnp.exp((o + 1.0) * logc), jnp.exp((BLK - 1.0 - o) * logc)
        keys, vals = slice(i * DK, (i + 1) * DK), slice(i * DVP, (i + 1) * DVP)
        after = later[i]
        for b in reversed(range(nb)):
            low = after.astype(BF16)
            dkey = gate[rows(b), keys] + contract(v_v[rows(b), vals], low, 1, 1) * to_end
            scaled = (k_v[rows(b), keys].astype(F32) * to_end).astype(BF16)
            dvalue = ret[rows(b), vals] + jnp.dot(scaled, low, preferred_element_type=F32)
            turned = turn(dkey, cos_ref[rows(b), :], -sin_ref[rows(b), :])
            dk[rows(b), keys] = (turned * (1.0 / math.sqrt(DK))).astype(BF16)
            dv[rows(b), vals] = dvalue.astype(BF16)
            if b > 0:
                qs = (q_v[rows(b), keys].astype(F32) * into).astype(BF16)
                after = decay_row(logc, DVP, float(BLK)) * after + contract(qs, dret[rows(b), vals], 0, 0)
    halves.append(send_half(2, dv, DVP, DVP))
    halves.append(send_half(3, dk, 2 * DVP + DK, DK))
    tokens_in.wait()
    for load in values_in:
        load.wait()

    spread, collect, pass_on, gather, drain_near, drain = reduce_scatter(scatter)
    ng_ref[...] = jnp.zeros_like(ng_ref)

    def side_copy(src, dst, sent, got, to):
        return pltpu.make_async_remote_copy(
            src_ref=src, dst_ref=dst, send_sem=sent, recv_sem=got, device_id={"head": to}, device_id_type=MESH,
        )

    def put(r):
        slot = lax.rem(r, 2)
        return pltpu.make_async_copy(s_gt.at[slot], gt_h.at[at(r)], gt_sem.at[slot])

    def step(t, carried):
        r1 = t - 1

        @pl.when((r1 >= 0) & (r1 < nr))
        def _():
            collect(r1)
            pass_on(r1)
            here = side.at[at(r1)]
            pltpu.make_async_copy(here, here, side_sem.at[r1]).wait()
            side_give[at(r1), :] += side[at(r1), :]
            side_copy(side_give.at[at(r1)], side_far.at[at(r1)], side_gone, side_got.at[r1], across).start()

        g = t - 2

        @pl.when(g >= 0)
        def _():
            grad = gather(g)
            here = side_far.at[at(g)]
            pltpu.make_async_copy(here, here, side_got.at[g]).wait()
            sums = (side_give[at(g), :] + side_far[at(g), :]) * (1.0 / D)
            normal, inverse = row_stats(rows_v[at(g), :].astype(F32), 1e-05)
            normal = own_block(normal)
            ng_ref[...] += jnp.sum(grad * normal, axis=0, keepdims=True)
            e = grad * own_block(gain_ref[0:1, :])
            result = dr_v[at(g), :] + inverse * (e - (sums[:, 0:1] + normal * sums[:, 1:2]))

            @pl.when(g >= 2)
            def _():
                put(g).wait()

            s_gt[lax.rem(g, 2)] = result.astype(BF16)
            put(g).start()

        @pl.when(t < nr)
        def _():
            terms = contract(dq[at(t), :], wq[...], 1, 1) + contract(dk[at(t), :], wk[...], 1, 1)
            terms = terms + jnp.dot(dv[at(t), :], big[...], preferred_element_type=F32)
            terms = terms + jnp.dot(dg[at(t), :], wg[...], preferred_element_type=F32)
            spread(t, terms)
            normal, _ = row_stats(rows_v[at(t), :].astype(F32), 1e-05)
            weighted = terms * gain_ref[0:1, :]
            plain = jnp.sum(weighted, axis=1, keepdims=True)
            cross = jnp.sum(weighted * normal, axis=1, keepdims=True)
            lane = lax.broadcasted_iota(jnp.int32, (ROWS, 128), 1)
            side_give[at(t), :] = jnp.where(lane == 0, plain, jnp.where(lane == 1, cross, 0.0))
            side_send(t).start()

        return carried

    def side_send(r):
        return side_copy(side_give.at[at(r)], side.at[at(r)], side_sent.at[r], side_sem.at[r], sibling)

    def guarded(t, carried):
        r1 = t - 1

        @pl.when((r1 >= 0) & (r1 < nr))
        def _():
            side_send(r1).wait_send()

        return step(t, carried)

    lax.fori_loop(0, nr + 2, guarded, 0)

    drain()
    pltpu.make_async_copy(side_give, side_far, side_gone).wait()
    for slot in range(2):
        put(slot).wait()
    for stay, go in halves:
        stay.wait()
        go.wait_send()
        go.wait_recv()
    mlp.wait()


def back_kernel(
    logc, grad_branch, w_output, retained, gate, group_gain, query, key, value, states, incoming,
    cosine, sine, w_query, w_key, wv, wg, all_tokens, gains, own_resid_grad, chip_sums, heads,
):
    T, D = all_tokens.shape
    cols, nr, nb = D // 4, T // ROWS, T // BLK
    keys, vals = heads * DK, heads * DVP
    low = functools.partial(jax.ShapeDtypeStruct, dtype=BF16)
    wide = functools.partial(jax.ShapeDtypeStruct, dtype=F32)
    anywhere, vmem = pl.BlockSpec(memory_space=pl.ANY), pl.BlockSpec(memory_space=pltpu.VMEM)
    dma = pltpu.SemaphoreType.DMA
    return pl.pallas_call(
        functools.partial(back_body, nr, heads),
        out_shape=[
            low((T, DVP * 2 + DK * 2)), low((T, DVP * 2 + DK * 2)), low((T, cols)),
            wide((1, vals)), low((T, cols)), wide((1, cols)),
        ],
        in_specs=[pl.BlockSpec(memory_space=pltpu.SMEM)] + [anywhere] * 4 + [vmem] + [anywhere] * 5
        + [vmem] * 2 + [anywhere] * 5 + [vmem, anywhere, anywhere],
        out_specs=[anywhere, anywhere, anywhere, vmem, anywhere, vmem],
        scratch_shapes=[
            pltpu.VMEM((T, D), BF16), pltpu.VMEM((vals, D), BF16), pltpu.VMEM((D, keys), BF16),
            pltpu.VMEM((D, keys), BF16), pltpu.VMEM((vals, D), BF16),
            pltpu.VMEM((T, vals), F32), pltpu.VMEM((T, vals), F32),
            pltpu.VMEM((T, keys), BF16), pltpu.VMEM((T, keys), BF16), pltpu.VMEM((T, vals), BF16),
            pltpu.VMEM((nb, heads, DK, DVP), F32), pltpu.VMEM((heads, DK, DVP), F32),
            pltpu.VMEM((T, cols), F32),
            pltpu.VMEM((T, vals), BF16), pltpu.VMEM((T, vals), BF16), pltpu.VMEM((T, keys), BF16),
            pltpu.VMEM((T, keys), BF16), pltpu.VMEM((T, vals), BF16),
            pltpu.VMEM((heads, DK, DVP), F32), pltpu.VMEM((heads, DK, DVP), F32),
            pltpu.VMEM((2, ROWS, cols), BF16),
            pltpu.VMEM((T, 128), F32), pltpu.VMEM((T, 128), F32), pltpu.VMEM((T, 128), F32),
            dma((11 + 2 * heads,)), dma((1 + heads,)), dma((4,)), dma((4,)), dma((2,)), dma((4,)), dma((2,)),
            dma((nr,)), dma((nr,)), dma((nr,)), dma,
        ] + carry_scratch() + scatter_scratch(T, D),
        compiler_params=pltpu.CompilerParams(
            collective_id=3, has_side_effects=True, vmem_limit_bytes=63 * 2**20
        ),
        cost_estimate=pl.CostEstimate(
            flops=2 * T * D * (2 * keys + 3 * vals), bytes_accessed=50 * 2**20, transcendentals=T * vals
        ),
        name="dbranch_to_grad_tokens",
    )(
        logc, grad_branch, w_output, retained, gate, group_gain, query, key, value, states, incoming,
        cosine, sine, w_query, w_key, wv, wg, all_tokens, gains, own_resid_grad, chip_sums,
    )


def pad_cols(w, parts):
    w = w.reshape(w.shape[0], parts, w.shape[1] // parts)
    fill = -w.shape[2] % 128
    return jnp.pad(w, ((0, 0), (0, 0), (0, fill))).reshape(w.shape[0], -1)


def pad_rows(w, parts):
    w = w.reshape(parts, w.shape[0] // parts, w.shape[1])
    fill = -w.shape[1] % 128
    return jnp.pad(w, ((0, 0), (0, fill), (0, 0))).reshape(-1, w.shape[2])


def unpad_rows(w, parts, real):
    return w.reshape(parts, -1, w.shape[1])[:, : real // parts].reshape(real, w.shape[1])


def seq_sum(grads):
    return [g.astype(F32) for g in lax.psum([g.astype(BF16) for g in grads], "seq")]


def unpad_cols(w, heads):
    return w.reshape(w.shape[0], heads, DVP)[:, :, :DV].reshape(w.shape[0], heads * DV)


def per_device(
    tokens,
    norm_gain,
    w_query,
    w_key,
    w_value,
    w_gate,
    group_gain,
    w_output,
    mlp_gain,
    w_first,
    w_second,
    w_third,
    cotangent,
):
    T, cols = tokens.shape
    heads = w_query.shape[1] // DK
    fast = lax.axis_size("seq") == 8 and lax.axis_size("head") == 4
    head_rank = lax.axis_index("head")
    seq_rank = lax.axis_index("seq")
    features = cols * lax.axis_size("head")

    units, values = w_first.shape[1], w_value.shape[1]
    if not fast:
        wv, wg, wo = pad_rows(w_value.T, heads), pad_rows(w_gate.T, heads), pad_rows(w_output, heads)
    gain = pad_cols(group_gain.astype(F32)[None], heads)

    positions = (seq_rank * T + jnp.arange(T)).astype(F32)
    frequency = 10000.0 ** (-jnp.arange(DK // 2, dtype=F32) / (DK // 2 - 1))
    angles = positions[:, None] * frequency[None, :]
    cosine, sine = jnp.cos(angles), jnp.sin(angles)
    head_ids = (head_rank * heads + jnp.arange(heads)).astype(F32)
    logc = jnp.log(1.0 - jnp.exp2(-5.0 - head_ids))
    factor = jnp.exp(T * logc)

    if fast:
        gains = jnp.concatenate([norm_gain[None], mlp_gain[None], jnp.zeros((6, cols), BF16)]).astype(F32)
        (
            all_tokens, all_cot, normed, far_normed, query, key, value, gate, retained, mixed, states,
            incoming, gains,
        ) = front_kernel(
            logc, tokens, cotangent, gains, w_query, w_key, w_value.T, w_gate.T, cosine, sine, gain, heads
        )
        full_mlp_gain = gains[1]
    else:
        gains = lax.all_gather(jnp.stack([norm_gain, mlp_gain]), "head", axis=1, tiled=True).astype(F32)
        full_gain, full_mlp_gain = gains[0], gains[1]
        all_tokens = lax.all_gather(tokens, "head", axis=1, tiled=True)
        all_cot = lax.all_gather(cotangent, "head", axis=1, tiled=True)
        normal_in, inverse_in = row_stats(all_tokens.astype(F32), 1e-05)
        normed = (normal_in * full_gain).astype(BF16)
        query_raw = jnp.dot(normed, w_query, preferred_element_type=F32)
        key_raw = jnp.dot(normed, w_key, preferred_element_type=F32)
        value = contract(normed, wv, 1, 1).astype(BF16)
        gate = contract(normed, wg, 1, 1)
        query, key, states = per_head(
            fwd_state_kernel, heads, T,
            ["smem", "key", "key", "val", "rot", "rot"],
            [("key", BF16), ("key", BF16), ("states", F32)],
            "retention_state",
        )(logc, query_raw, key_raw, value, cosine, sine)
        incoming = seq_carry(states[-1], factor, False)
        mixed, retained = per_head(
            fwd_out_kernel, heads, T,
            ["smem", "key", "key", "val", "states", "state", "val", "gain"],
            [("val", BF16), ("val", F32)],
            "retention_out",
        )(logc, query, key, value, states, incoming, gate, gain)

    middle = middle_kernel if fast else middle_general
    (
        normed_two, hidden, grad_up_one, grad_up_two, output, chip_sums, grad_branch, own_resid_grad, far_two,
        far_up_one, far_up_two, mlp_gain_grad,
    ) = middle(
        mixed, all_tokens, all_cot, w_output, w_first.T, w_second.T, w_third, full_mlp_gain[None], heads,
    )
    grad_mlp_gain = lax.dynamic_slice_in_dim(mlp_gain_grad[0], head_rank * cols, cols)

    if fast:
        near, far, far_sums, group_gain_grad, grad_tokens, grad_norm_gain = back_kernel(
            logc, grad_branch, w_output, retained, gate, gain, query, key, value, states, incoming,
            cosine, sine, w_query, w_key, w_value.T, w_gate.T, all_tokens, gains, own_resid_grad, chip_sums, heads,
        )
        output = output + (chip_sums[:, cols:].astype(F32) + far_sums.astype(F32))
        small = jnp.concatenate([grad_norm_gain[0], group_gain_grad[0], grad_mlp_gain])[None].astype(BF16)
        full = chain_sum(
            jnp.pad(small, ((0, 15), (0, 0))), hidden, all_cot, mixed, grad_branch, grad_up_one, grad_up_two,
            far_up_one, far_up_two, normed_two, far_two, near, far, normed, far_normed,
        )
        (
            small, grad_third, grad_first, grad_second, grad_output, grad_gate, grad_value, grad_query, grad_key,
        ) = finish(full, [(i * DV, DV, False) for i in range(2, 7)] + [(7 * DV, DK, True), (7 * DV + DK, DK, True)])
        small = small[0]
    else:
        grad_mixed = contract(grad_branch, wo, 1, 1)
        grad_gate_rows, grad_ret, group_gain_grad, state_grad = per_head(
            bwd_mix_kernel, heads, T,
            ["smem", "val", "val", "val", "gain", "key"],
            [("val", BF16), ("val", BF16), ("gain", F32), ("state", F32)],
            "mix_backward",
        )(logc, grad_mixed, retained, gate, gain, query)
        outgoing = seq_carry(state_grad, factor, True)
        grad_query_raw, grad_key_raw, grad_value_rows = per_head(
            bwd_ret_kernel, heads, T,
            ["smem", "key", "key", "val", "val", "states", "state", "state", "rot", "rot"],
            [("key", BF16), ("key", BF16), ("val", BF16)],
            "retention_backward",
        )(logc, query, key, value, grad_ret, states, incoming, outgoing, cosine, sine)
        input_terms = (
            contract(grad_query_raw, w_query, 1, 1)
            + contract(grad_key_raw, w_key, 1, 1)
            + jnp.dot(grad_value_rows, wv, preferred_element_type=F32)
            + jnp.dot(grad_gate_rows, wg, preferred_element_type=F32)
        )
        grad_normed = head_reduce_scatter(input_terms)
        weighted = input_terms * full_gain
        sums = lax.psum(
            jnp.stack([jnp.sum(weighted, axis=1), jnp.sum(weighted * normal_in, axis=1)]), "head"
        )
        own_normal = lax.dynamic_slice_in_dim(normal_in, head_rank * cols, cols, axis=1)
        scaled_grad = grad_normed * norm_gain.astype(F32)
        grad_tokens = (
            own_resid_grad
            + inverse_in
            * (scaled_grad - (sums[0][:, None] + own_normal * sums[1][:, None]) / features)
        ).astype(BF16)
        grad_norm_gain = jnp.sum(grad_normed * own_normal, axis=0)
        grads = [contract(act, normed, 0, 0) for act in (grad_query_raw, grad_key_raw)]
        grads += [
            unpad_rows(contract(grad_value_rows, normed, 0, 0), heads, values),
            unpad_rows(contract(grad_gate_rows, normed, 0, 0), heads, values),
            unpad_rows(contract(mixed, grad_branch, 0, 0), heads, values),
            unpad_rows(contract(hidden, all_cot, 0, 0), heads, units),
            unpad_rows(contract(grad_up_one, normed_two, 0, 0), heads, units),
            unpad_rows(contract(grad_up_two, normed_two, 0, 0), heads, units),
        ]
        (
            grad_query, grad_key, grad_value, grad_gate, grad_output, grad_third, grad_first, grad_second,
        ) = seq_sum(grads)
        grad_query, grad_key = grad_query.T, grad_key.T
        small = lax.psum(jnp.concatenate([grad_norm_gain, group_gain_grad[0], grad_mlp_gain]), "seq")

    grad_norm_gain = small[:cols]
    grad_group_gain = unpad_cols(small[None, cols : cols + heads * DVP], heads)[0]
    grad_mlp_gain = small[cols + heads * DVP :]
    return (
        output.astype(BF16),
        grad_tokens,
        grad_norm_gain,
        grad_query,
        grad_key,
        grad_value.T,
        grad_gate.T,
        grad_group_gain,
        grad_output,
        grad_mlp_gain,
        grad_first.T,
        grad_second.T,
        grad_third,
    )


def solution(mesh):
    rows_cols, cut, columns, depth = P("seq", "head"), P("head"), P(None, "head"), P("head", None)
    return jax.shard_map(
        per_device,
        mesh=mesh,
        in_specs=(
            rows_cols, cut, columns, columns, columns, columns, cut, depth, cut,
            columns, columns, depth, rows_cols,
        ),
        out_specs=(
            rows_cols, rows_cols, cut, columns, columns, columns, columns, cut, depth, cut,
            columns, columns, depth,
        ),
        check_vma=False,
    )
```

time: 1720 us -> 706 us (0.41)
  waiting for transfers between devices: 1050 us -> 0 us
  Pallas kernels: 0 us -> 680 us
  matrix products: 235 us -> 0 us
  local copies, waits for them, and re-layouts: 196 us -> 8.67 us
  other arithmetic: 126 us -> 8.49 us
  blocking collectives: 79.1 us -> 0 us
    psum x2 -> x0, waiting for transfers between devices: 819 us -> none  [the longest x1 734 us: per_device(): lax.psum(grad_query.astype(jnp.bfloat16), 'seq').astype(jnp.float32)]
    pallas_call x0 -> x5, Pallas kernels: none -> 680 us  [the longest x1 351 us: chain_sum(): pl.pallas_call(functools.partial(chain_kernel, chunks // 2), out_shape=ja...]
    dot_general x48 -> x0, matrix products: 235 us -> none  [the longest x16 110 us: contract(): lax.dot_general(left_side, right_side, (((left_dim,), (right_dim,)), ((),...]
    all_gather x5 -> x0, waiting for transfers between devices: 189 us -> none  [the longest x1 80.9 us: prefix(): pieces = jax.tree.map(lambda part: lax.all_gather(part, axis), value)]
    dynamic_update_slice x10 -> x0, local copies, waits for them, and re-layouts: 77.6 us -> none  [the longest x4 70.8 us: local_forward(): lax.scan(one_block, initial_state, (split_blocks(queries), split_blocks(k...]
    all_gather x4 -> x0, blocking collectives: 52.9 us -> none  [the longest x1 20.8 us: prefix(): pieces = jax.tree.map(lambda part: lax.all_gather(part, axis), value)]
    dynamic_slice x55 -> x0, local copies, waits for them, and re-layouts: 49.9 us -> none  [the longest x14 32.3 us: prefix_lap(): longer = join(total, jax.tree.map(lambda part: part[position], pieces))]
    reduce_scatter x3 -> x0, waiting for transfers between devices: 42.8 us -> none  [the longest x1 42.8 us: per_device(): lax.psum_scatter(branch_terms.astype(jnp.bfloat16), 'head', scatter_dimen...]
  transfers between devices with their start and end apart: 10 -> 0, of which waited for: 8 -> 0; matrix products, arithmetic and copies ran while one was open for 13% -> 0% of each run, Pallas kernels for 0% -> 0%
where the time goes in v1:
time: 706 us; the launch traced here: 698 us
  Pallas kernels  680 us (96%)
  local copies, waits for them, and re-layouts  8.67 us (1%)
  other arithmetic  8.49 us (1%)
    pallas_call x1, Pallas kernels, chain_sum(): pl.pallas_call(functools.partial(chain_kernel, chunks // 2), out_shape=ja...  351 us
    pallas_call x1, Pallas kernels, middle_kernel(): pl.pallas_call(functools.partial(middle_body, nr, heads), out_shape=[low(...  119 us
    pallas_call x1, Pallas kernels, back_kernel(): pl.pallas_call(functools.partial(back_body, nr, heads), out_shape=[low((T...  102 us
    pallas_call x1, Pallas kernels, front_kernel(): pl.pallas_call(functools.partial(front_body, nr, heads), out_shape=[low((...  80.4 us
    pallas_call x1, Pallas kernels, finish(): pl.pallas_call(functools.partial(finish_kernel, layout), grid=(D // tile,...  27.5 us

profile of v1, /device:TPU:0, one launch (start us, length us, event | category | flops | bytes accessed | tf_op | source)
XLA Modules:
  0.0 698.3 jit_solution(16589071926971386781)
XLA Ops:
  0.7 0.5 subtract_log_fusion.logc_ref
  1.2 0.1 pad.16.clone
  1.3 0.7 broadcast_in_dim.12
  2.0 0.8 reshape_broadcast_in_dim.7
  2.7 0.6 copy.26
  3.3 0.7 broadcast_in_dim.13
  4.0 0.7 maximum_convert_fusion.gains_ref
  4.7 3.0 multiply_sine_fusion
  7.7 80.4 %tokens_to_mixed.1 = (bf16[1024,2048]{1,0:T(8,128)(2,1)}, bf16[1024,2048]{1,0:T(8,128)(2,1)}, bf16[1024,2048]{1,0:T(8,128)(2,1)}, bf16[1024,2048]{1,0:T(8,128)(2...) custom-call(f32[2]{0:T(128)} %subtract_log_fusion.logc_ref, ...), custom_call_target="tpu_custom_call" | custom-call | flops 12884901888 | bytes 62914560 | tf_op jit(solution)/shard_map/tokens_to_mixed/pallas_call | solution.py:1332
  88.1 1.4 slice.29.gain_ref
  89.6 119.3 %mixed_to_dbranch.1 = (bf16[1024,2048]{1,0:T(8,128)(2,1)}, bf16[1024,1024]{1,0:T(8,128)(2,1)}, bf16[1024,1024]{1,0:T(8,128)(2,1)}, bf16[1024,1024]{1,0:T(8,128)(...) custom-call(bf16[1024,1024]{1,0:T(8,128)(2,1)} %get-tuple-element.53, ...), custom_call_target="tpu_custom_call" | custom-call | flops 30064771072 | bytes 52428800 | tf_op jit(solution)/shard_map/mixed_to_dbranch/pallas_call | solution.py:951
  208.8 102.0 %dbranch_to_grad_tokens.1 = (bf16[1024,1536]{1,0:T(8,128)(2,1)}, bf16[1024,1536]{1,0:T(8,128)(2,1)}, bf16[1024,512]{1,0:T(8,128)(2,1)}, f32[1,1024]{1,0:T(1,128)...) custom-call(f32[2]{0:T(128)} %subtract_log_fusion.logc_ref, bf16[1024,2048]{1,0:T(8,128)(2,1)} %get-tuple-element.59.db_h.branch_h, ...), custom_call_target="tpu_custom_call" | custom-call | flops 17179869184 | bytes 52428800 | tf_op jit(solution)/shard_map/dbranch_to_grad_tokens/pallas_call | solution.py:1603
  310.9 0.0 copy-start.2
  310.9 0.0 copy-start.1
  310.9 3.6 add_convert_fusion
  314.5 0.7 dynamic-slice_convert_fusion
  315.1 0.0 copy-done.2
  315.1 0.0 copy-done.1
  315.1 0.6 fusion.4.small_h
  315.8 350.7 %gradient_chains.1.full_ref = bf16[2,3552,2048]{2,1,0:T(8,128)(2,1)} custom-call(bf16[16,2048]{1,0:T(8,128)(2,1)} %fusion.4.small_h, bf16[1024,1024]{1,0:T(8,128)(2,1)} %get-tuple-element.73.hid_h, bf16[1024,2048]{1,0:T(8,128)(2,1)} %get-tuple-element.55.cot_h, bf16[1024,1024]{1,0:T(8,128)(2,1)} %get-tuple-element.53.mixed_h, ...), custom_call_target="tpu_custom_call" | custom-call | tf_op jit(solution)/shard_map/gradient_chains/pallas_call | solution.py:339
  666.5 0.0 copy-start
  666.5 27.5 %gradients_to_float32.1 = (f32[8,2048]{1,0:T(8,128)}, f32[864,2048]{1,0:T(8,128)}, f32[864,2048]{1,0:T(8,128)}, f32[864,2048]{1,0:T(8,128)}, f32[864,2048]{1,0:T...) custom-call(bf16[2,3552,2048]{2,1,0:T(8,128)(2,1)} %gradient_chains.1.full_ref), custom_call_target="tpu_custom_call" | custom-call | tf_op jit(solution)/shard_map/gradients_to_float32/pallas_call | solution.py:388
  694.1 0.8 slice_reduce_fusion
  694.9 1.3 fusion.5
  696.2 0.7 squeeze_reshape.3
  696.9 0.0 copy-done
  696.9 1.0 copy.28
  (7 shorter events, 0.0 us)
Async XLA Ops:
  310.9 4.3 copy-start.2
  310.9 4.3 copy-start.1
  666.5 30.3 %copy-start = (bf16[1024,512]{1,0:T(8,128)(2,1)S(1)}, bf16[1024,512]{1,0:T(8,128)(2,1)}, u32[]{:S(2)}) copy-start(bf16[1024,512]{1,0:T(8,128)(2,1)} %get-tuple-element.111) | copy-start | bytes 3145732
